TPU v7x, 128 devices: a whole 4x4x4 slice. The times are simulated.
128 devices in a mesh: ctx: 16 (over x_lo, y, core), ch: 8 (over z, x_hi).
Axes of the slice: x: 4 (x_hi: 2, x_lo: 2; x = x_hi * 2 + x_lo), y: 4, z: 4, core: 2. Of those that a mesh axis runs over, the one named last changes fastest.
Arguments:
- hidden: bfloat16 [8192, 4096], P('ctx', 'ch'), may hold values from -6 to 6
- norm_gain: float32 [2, 4096], replicated, may hold values from 0.5 to 2
- in_weight: bfloat16 [2, 4096, 3, 4096], P(None, 'ctx', None, 'ch'), may hold values from -0.09375 to 0.09375
- feat_filter: float32 [2, 3, 3, 4096], P(None, None, None, 'ch'), may hold values from -3 to 3
- se_filter: float32 [7, 4096], P(None, 'ch'), may hold values from -2 to 2
- mr_filter: float32 [128, 4096], P(None, 'ch'), may hold values from -0.5 to 0.5
- skip_gain: float32 [2, 4096], P(None, 'ch'), may hold values from -1 to 1
- out_weight: bfloat16 [2, 4096, 4096], P(None, 'ch', 'ctx'), may hold values from -0.125 to 0.125
Outputs:
- result: bfloat16 [8192, 4096], P('ctx', 'ch')
All inputs are finite; a program needn't handle non-finite values.
Results may differ from a plain program's by a relative error of at most 0.04.
Values may be sent and summed in bfloat16 or wider, within the bound.
No kernel may reach another device: no remote copies, remote signals or barrier semaphores. Data moves between devices by JAX's collectives and lax.ppermute only.
A program may use at most 128 MiB of HBM per device.

v0:
```python
import functools

import jax
import jax.numpy as jnp
import numpy as np
from jax import lax
from jax.experimental.layout import Layout, with_layout_constraint
from jax.experimental import pallas as pl
from jax.experimental.pallas import tpu as pltpu
from jax.sharding import Mesh, PartitionSpec as P

AXES = ("xl", "y", "core", "z", "xh")
HALF = 256
CUT = 1152
LANES = 128


def shift(value, axis, by):
    size = lax.axis_size(axis)
    return lax.ppermute(value, axis, [(i, (i + by) % size) for i in range(size)])


def swap(value):
    moved = lax.ppermute(value, ("core", "xh"), [(1, 2), (2, 1)])
    same = lax.axis_index("core") == lax.axis_index("xh")
    return jnp.where(same, value, moved)


def from_behind(value, axes):
    return lax.ppermute(value, axes, [(i, i + 1) for i in range(15)])


def by_rows(value):
    return with_layout_constraint(value, Layout(major_to_minor=tuple(range(value.ndim))))


def after(value, *others):
    return lax.optimization_barrier((value, *others))[0]


def together(*values):
    return lax.optimization_barrier(values)


def fetch(moves, sources, target, index_ref, semaphores):
    copies = []
    for number, (source, lead, lane, width, slot, other, by_rows, *fixed) in enumerate(moves):
        block = fixed[0] * 256 if slot is None else pl.multiple_of(index_ref[slot] * 256, 256)
        ref = sources[source]
        if lead is not None:
            ref = ref.at[lead]
        if by_rows:
            piece = target.at[pl.ds(block, 256), other : other + width]
        else:
            piece = target.at[other : other + ref.shape[0], pl.ds(block, 256)]
        copies.append(pltpu.make_async_copy(ref.at[:, lane : lane + width], piece, semaphores.at[number]))
    return copies


def norm_pieces(loads, places, raw, gain_ref, normed, squares):
    squares[...] = jnp.zeros_like(squares)
    for j, load in enumerate(loads):
        load.wait()
        lanes = pl.ds(pl.multiple_of(places[j] * 512, 512), 512)
        gain = gain_ref[pl.ds(places[j], 1), :]

        @pl.loop(0, squares.shape[0] // 64)
        def _(step):
            rows = pl.ds(pl.multiple_of(step * 64, 64), 64)
            x = raw[j, rows, :].astype(jnp.float32)
            normed[rows, lanes] = (x * gain).astype(jnp.bfloat16)
            q = x * x
            squares[rows, :] += (q[:, :128] + q[:, 128:256]) + (q[:, 256:384] + q[:, 384:])

    squares[:, :1] = lax.rsqrt(jnp.sum(squares[...], axis=1, keepdims=True) * (1.0 / 4096) + 1e-06)


def norm_kernel(index_ref, gain_ref, *refs):
    xs, (normed, squares, raw, x_sems) = refs[:-4], refs[-4:]
    xs = [xs[0].at[j] for j in range(8)] if len(xs) == 1 else xs
    loads = [pltpu.make_async_copy(x, raw.at[j], x_sems.at[j]) for j, x in enumerate(xs)]
    for load in loads:
        load.start()
    norm_pieces(loads, [index_ref[j] for j in range(8)], raw, gain_ref, normed, squares)


def norm_rows(index, gain, pieces):
    rows = pieces[0].shape[-2]
    any_space = pl.BlockSpec(memory_space=pl.ANY)
    vmem = pl.BlockSpec(memory_space=pltpu.VMEM)
    return pl.pallas_call(
        norm_kernel,
        out_shape=[
            jax.ShapeDtypeStruct((rows, 4096), jnp.bfloat16),
            jax.ShapeDtypeStruct((rows, LANES), jnp.float32),
        ],
        in_specs=[pl.BlockSpec(memory_space=pltpu.SMEM), vmem] + [any_space] * len(pieces),
        out_specs=[vmem, vmem],
        scratch_shapes=[pltpu.VMEM((8, rows, 512), jnp.bfloat16), pltpu.SemaphoreType.DMA((8,))],
        compiler_params=pltpu.CompilerParams(vmem_limit_bytes=24 * 1024 * 1024),
        cost_estimate=pl.CostEstimate(flops=rows * 4096 * 4, bytes_accessed=rows * 4096 * 4, transcendentals=0),
    )(index, gain, *pieces)


def in_kernel(moves, groups, halo, index_ref, *refs):
    ins, refs = refs[: 2 * groups], refs[2 * groups :]
    count = 1 + max(m[0] for m in moves)
    ws, refs = refs[:count], refs[count:]
    out_refs, (tail_ref, weights, w_sems) = refs[:2], refs[2:]
    copies = fetch(moves, ws, weights, index_ref, w_sems)
    for copy in copies:
        copy.start()
    for copy in copies:
        copy.wait()

    @pl.loop(0, 6)
    def _(step):
        lanes = pl.ds(pl.multiple_of(step * 256, 256), 256)
        for group in range(groups):
            normed, squares = ins[2 * group], ins[2 * group + 1]
            product = jnp.dot(normed[...], weights[:, lanes], preferred_element_type=jnp.float32)
            product = (product * squares[:, :1]).astype(jnp.bfloat16)
            for part in range(2 // groups):
                out_refs[group + part][:, lanes] = product[part * HALF : (part + 1) * HALF]

    last = out_refs[-1]
    tail_ref[:halo, :] = last[HALF - halo :, 512:]
    tail_ref[halo:, :512] = last[HALF - 16 :, :512]
    tail_ref[halo:, 512:] = jnp.zeros((16, 512), jnp.bfloat16)


def project_in(index, rows, weights, moves, halo):
    any_space = pl.BlockSpec(memory_space=pl.ANY)
    vmem = pl.BlockSpec(memory_space=pltpu.VMEM)
    return pl.pallas_call(
        functools.partial(in_kernel, moves, len(rows) // 2, halo),
        out_shape=[jax.ShapeDtypeStruct((HALF, 1536), jnp.bfloat16)] * 2
        + [jax.ShapeDtypeStruct((halo + 16, 1024), jnp.bfloat16)],
        in_specs=[pl.BlockSpec(memory_space=pltpu.SMEM)] + [vmem] * len(rows) + [any_space] * len(weights),
        out_specs=[vmem] * 3,
        scratch_shapes=[pltpu.VMEM((4096, 1536), jnp.bfloat16), pltpu.SemaphoreType.DMA((len(moves),))],
        compiler_params=pltpu.CompilerParams(vmem_limit_bytes=48 * 1024 * 1024),
        cost_estimate=pl.CostEstimate(flops=4 * HALF * 4096 * 1536, bytes_accessed=18 * 2**20, transcendentals=0),
    )(index, *rows, *weights)


def filter_rows(halo, taps, before_ref, main_ref, feat_ref, filter_ref, skip_ref, inner, shaped, gated, copies8):
    total = halo + HALF

    if before_ref.shape[1] == 1024:
        shaped[:16, :512] = before_ref[halo:, :512].astype(jnp.float32)
        shaped[:halo, 512:] = before_ref[:halo, :].astype(jnp.float32)
    else:
        shaped[:16, :512] = before_ref[HALF - 16 :, :512].astype(jnp.float32)
        shaped[:halo, 512:] = before_ref[HALF - halo :, 512:].astype(jnp.float32)
    shaped[16 : 16 + HALF, :512] = main_ref[:, :512].astype(jnp.float32)
    shaped[halo:total, 512:] = main_ref[:, 512:].astype(jnp.float32)

    def feature(start, size, s, lanes):
        value = None
        for j in range(3):
            tap = feat_ref[3 * j + s : 3 * j + s + 1, lanes]
            low = s * 512 + lanes.start
            term = tap * shaped[start - j : start - j + size, low : low + LANES]
            value = term if value is None else value + term
        return value

    for lane in range(0, 512, LANES):
        lanes = slice(lane, lane + LANES)
        for start in range(8, total, 64):
            size = min(64, total - start)
            gated[start : start + size, lanes] = feature(start, size, 1, lanes) * feature(start, size, 2, lanes)
        gated[:8, lanes] = jnp.zeros((8, LANES), jnp.float32)

    if taps == 7:
        for lane in range(0, 512, LANES):
            lanes = slice(lane, lane + LANES)
            for start in range(0, HALF, 64):
                own = gated[halo + start : halo + start + 64, lanes]
                value = (skip_ref[:1, lanes] + filter_ref[:1, lanes]) * own
                for j in range(1, taps):
                    value = value + filter_ref[j : j + 1, lanes] * gated[halo + start - j : halo + start - j + 64, lanes]
                inner[start : start + 64, lanes] = (feature(16 + start, 64, 0, lanes) * value).astype(jnp.bfloat16)
    else:
        for lane in range(0, 512, LANES):
            lanes = slice(lane, lane + LANES)
            for r in range(8):
                for start in range(0, HALF + 128, 128):
                    copies8[r, start : start + 128, :] = gated[16 + start - r : 16 + start - r + 128, lanes]

            @pl.loop(0, HALF // 128)
            def _(step):
                base = pl.multiple_of(step * 128, 128)
                value = jnp.zeros((128, LANES), jnp.float32)
                for r in range(8):
                    for a in range(0, 16, 4):
                        window = copies8[r, pl.ds(pl.multiple_of(base + 128 - 8 * (a + 3), 8), 128 + 24), :]
                        for b in range(4):
                            tap = filter_ref[8 * (a + b) + r : 8 * (a + b) + r + 1, lanes]
                            low = 8 * (3 - b)
                            value = value + tap * window[low : low + 128]
                copies8[8, pl.ds(base, 128), :] = value

            for start in range(0, HALF, 64):
                own = gated[halo + start : halo + start + 64, lanes]
                value = copies8[8, start : start + 64, :] + skip_ref[:1, lanes] * own
                inner[start : start + 64, lanes] = (feature(16 + start, 64, 0, lanes) * value).astype(jnp.bfloat16)


def product_rows(outs, index_ref, inner, weights, out_refs):
    z = index_ref[0]
    core = index_ref[1]
    for by in range(4):
        block = lax.rem(z + by, 4)
        if outs == 4:
            columns = pl.ds(pl.multiple_of(block * 1024, 1024), 1024)
            out_refs[by][...] = jnp.dot(
                inner[...], weights[:, columns], preferred_element_type=jnp.float32
            ).astype(jnp.bfloat16)
        else:
            for side in range(2):
                place = block * 2 + (core if side == 0 else 1 - core)
                columns = pl.ds(pl.multiple_of(place * 512, 512), 512)
                out_refs[side][by] = jnp.dot(
                    inner[...], weights[:, columns], preferred_element_type=jnp.float32
                ).astype(jnp.bfloat16)


def filter_scratch(halo, taps):
    return [
        pltpu.VMEM((halo + HALF + 16, 1536), jnp.float32),
        pltpu.VMEM((halo + HALF, 512), jnp.float32),
        pltpu.VMEM((9, 8, LANES) if taps == 7 else (9, HALF + 128, LANES), jnp.float32),
    ]


def mix_kernel(moves, halo, taps, outs, index_ref, before_ref, main_ref, feat_ref, filter_ref, skip_ref, *refs):
    count = 1 + max(m[0] for m in moves)
    ws, refs = refs[:count], refs[count:]
    out_refs, refs = refs[:outs], refs[outs:]
    shaped, gated, copies8, inner, weights, w_sems = refs
    copies = fetch(moves, ws, weights, index_ref, w_sems)
    for copy in copies:
        copy.start()
    filter_rows(halo, taps, before_ref, main_ref, feat_ref, filter_ref, skip_ref, inner, shaped, gated, copies8)
    for copy in copies:
        copy.wait()
    product_rows(outs, index_ref, inner, weights, out_refs)


def mix_out(index, before, main, feat, taps, skip, weights, moves, halo, out_shapes):
    any_space = pl.BlockSpec(memory_space=pl.ANY)
    vmem = pl.BlockSpec(memory_space=pltpu.VMEM)
    length = taps.shape[0]
    return pl.pallas_call(
        functools.partial(mix_kernel, moves, halo, length, len(out_shapes)),
        out_shape=[jax.ShapeDtypeStruct(s, jnp.bfloat16) for s in out_shapes],
        in_specs=[pl.BlockSpec(memory_space=pltpu.SMEM)] + [vmem] * 5 + [any_space] * len(weights),
        out_specs=[vmem] * len(out_shapes),
        scratch_shapes=filter_scratch(halo, length)
        + [
            pltpu.VMEM((HALF, 512), jnp.bfloat16),
            pltpu.VMEM((512, 4096), jnp.bfloat16),
            pltpu.SemaphoreType.DMA((len(moves),)),
        ],
        compiler_params=pltpu.CompilerParams(vmem_limit_bytes=48 * 1024 * 1024),
        cost_estimate=pl.CostEstimate(flops=2 * HALF * 512 * 4096, bytes_accessed=6 * 2**20, transcendentals=0),
    )(index, before, main, feat, taps, skip, *weights)


def filter_kernel(halo, taps, before_ref, main_ref, feat_ref, filter_ref, skip_ref, inner, shaped, gated, copies8):
    filter_rows(halo, taps, before_ref, main_ref, feat_ref, filter_ref, skip_ref, inner, shaped, gated, copies8)


def filtered(before, main, feat, taps, skip, halo):
    vmem = pl.BlockSpec(memory_space=pltpu.VMEM)
    length = taps.shape[0]
    return pl.pallas_call(
        functools.partial(filter_kernel, halo, length),
        out_shape=jax.ShapeDtypeStruct((HALF, 512), jnp.bfloat16),
        in_specs=[vmem] * 5,
        out_specs=vmem,
        scratch_shapes=filter_scratch(halo, length),
        compiler_params=pltpu.CompilerParams(vmem_limit_bytes=24 * 1024 * 1024),
        cost_estimate=pl.CostEstimate(flops=2 * HALF * 512 * 4096 * 3, bytes_accessed=3 * 2**20, transcendentals=0),
    )(before, main, feat, taps, skip)


def product_kernel(moves, outs, index_ref, inner, weight_ref, *refs):
    out_refs, (weights, w_sems) = refs[:outs], refs[outs:]
    copies = fetch(moves, [weight_ref], weights, index_ref, w_sems)
    for copy in copies:
        copy.start()
    for copy in copies:
        copy.wait()
    product_rows(outs, index_ref, inner, weights, out_refs)


def project_out(index, inner, weight, moves, out_shapes):
    vmem = pl.BlockSpec(memory_space=pltpu.VMEM)
    return pl.pallas_call(
        functools.partial(product_kernel, moves, len(out_shapes)),
        out_shape=[jax.ShapeDtypeStruct(s, jnp.bfloat16) for s in out_shapes],
        in_specs=[pl.BlockSpec(memory_space=pltpu.SMEM), vmem, pl.BlockSpec(memory_space=pl.ANY)],
        out_specs=[vmem] * len(out_shapes),
        scratch_shapes=[pltpu.VMEM((512, 4096), jnp.bfloat16), pltpu.SemaphoreType.DMA((len(moves),))],
        compiler_params=pltpu.CompilerParams(vmem_limit_bytes=48 * 1024 * 1024),
        cost_estimate=pl.CostEstimate(flops=2 * HALF * 512 * 4096, bytes_accessed=6 * 2**20, transcendentals=0),
    )(index, inner, weight)


def per_device(hidden, norm_gain, in_weight, feat_filter, se_filter, mr_filter, skip_gain, out_weight):
    xl, y, core, z, xh = (lax.axis_index(a) for a in AXES)
    behind = lambda place, by: (place - by) % 4
    gains = norm_gain.reshape(2, 8, 512)
    ways = (1, -1, 2)
    other_core = lambda value: shift(value, "core", 1)
    gather = lambda value, axes: by_rows(lax.all_gather(by_rows(value), axes, axis=0, tiled=False))

    side_by_side = lambda w, o: jnp.concatenate([w.reshape(256, 1536), o[:256], o[256:]], axis=1)

    whole = lax.all_gather(hidden, ("z", "xh"), axis=0, tiled=False)

    m = side_by_side(in_weight[0], out_weight[0])
    m_xl = shift(m, "xl", 1)
    m_xl, w1, *m_y = together(m_xl, swap(in_weight[1]), *[shift(m, "y", by) for by in ways])
    o1 = swap(after(out_weight[1], m_xl))
    rest = shift(jnp.stack([v[:, CUT:] for v in m_y]), "xl", 1)
    most = [shift(m_xl[:, :CUT], "y", by) for by in ways]
    rest, *more = together(rest, *most, *[other_core(after(v, most[0])) for v in (m, m_xl, *m_y)])
    most, far = more[:3], more[3:]
    w_list = [m, m_xl, *m_y, *far, rest, *most] + [other_core(v) for v in (rest, *most)]
    w_moves, q_moves, slots = [], [], [z, core]

    def take(number, lead, at_xl, at_y, at_core, low, high):
        w_moves.append((number, lead, 0, min(high, 1536) - low, len(slots), low, True))
        if high == 2048:
            for half in range(2):
                q_moves.append((number, lead, 1536 + 256 * half - low, 256, len(slots), 256 * half, False))
        slots.append(at_xl * 8 + at_y * 2 + at_core)

    for number, c in ((0, core), (5, 1 - core)):
        take(number, None, xl, y, c, 0, 2048)
        take(number + 1, None, 1 - xl, y, c, 0, 2048)
        for e, by in enumerate(ways):
            take(number + 2 + e, None, xl, behind(y, by), c, 0, 2048)
    for number, c in ((10, core), (14, 1 - core)):
        for e, by in enumerate(ways):
            take(number, e, 1 - xl, behind(y, by), c, CUT, 2048)
            take(number + 1 + e, None, 1 - xl, behind(y, by), c, 0, CUT)
    q_index = jnp.stack(slots).astype(jnp.int32)
    q_list = w_list[:15]

    w1 = gather(after(side_by_side(w1, o1), rest, *most), ("xh", "xl", "y"))
    small = jnp.concatenate([feat_filter[1].reshape(9, 512), skip_gain[1:2], mr_filter], axis=0)

    rows = norm_rows(jnp.arange(8, dtype=jnp.int32), gains[0], [whole])
    low, high, tail = project_in(q_index, rows, w_list, w_moves, 16)
    base, small = after((hidden, small), low)
    base, small = swap(base), swap(small)
    tail = from_behind(tail, ("xl", "y", "core"))

    def first_parts(before, main):
        parts = mix_out(
            q_index, before, main, feat_filter[0].reshape(9, 512), se_filter, skip_gain[0:1], q_list, q_moves, 16,
            [(HALF, 1024)] * 4,
        )
        return parts[0], [shift(part, "z", by) for by, part in ((1, parts[1]), (-1, parts[3]), (2, parts[2]))]

    def over_z(own, received):
        total = own.astype(jnp.float32)
        for value in received:
            total = total + value.astype(jnp.float32)
        total = total.astype(jnp.bfloat16)
        pick = lambda c: jnp.where(c == 0, total[:, :512], total[:, 512:])
        mine, others = pick(core), pick(1 - core)
        return mine, [
            lax.ppermute(mine, ("core", "xh"), [(1, 0), (2, 3)]),
            lax.ppermute(others, ("core", "xh"), [(1, 2), (2, 1)]),
            lax.ppermute(others, ("core", "xh"), [(0, 2), (3, 1)]),
        ]

    def over_x(mine, received, rows):
        kept = jnp.where(core == xh, mine, jnp.zeros_like(mine))
        current = base[rows : rows + HALF].astype(jnp.float32) + kept.astype(jnp.float32)
        for value in received:
            current = current + value.astype(jnp.float32)
        return current.astype(jnp.bfloat16)

    own_high, high_z = first_parts(low, high)
    own_low, low_z = first_parts(tail, low)
    mine_high, high_x = over_z(own_high, high_z)
    *low_z, one, two, three = together(*low_z, *high_x)
    high = over_x(mine_high, (one, two, three), HALF)
    mine_low, low_x = over_z(own_low, low_z)
    high_near = [shift(high, "z", by) for by in ways]
    one, two, three, *high_near = together(*low_x, *high_near)
    low = over_x(mine_low, (one, two, three), 0)

    places = [(p, (p // 4 % 2) * 8 + (p % 4) * 2 + p // 8) for p in range(16)]
    w_moves = [(0, p, 0, 1536, None, 0, True, block) for p, block in places]
    p_moves = [(0, p, 1536 + 256 * half, 256, None, 256 * half, False, block) for p, block in places for half in range(2)]
    x_index = jnp.stack([behind(z, by) * 2 + c for c in (core, 1 - core) for by in (0, *ways)]).astype(jnp.int32)

    def normed(near):
        return norm_rows(x_index, gains[1], near + [other_core(v) for v in near])

    high_near = [high] + high_near
    low_near = [low] + [shift(low, "z", by) for by in ways]
    rows = normed(low_near) + normed(high_near)
    p_low, p_high, tail = project_in(q_index, rows, [w1], w_moves, 144)
    tail = from_behind(tail, ("xl", "y", "xh"))

    def second_filter(before, main):
        return filtered(before, main, small[:9], small[10:], small[9:10], 144)

    def second_parts(inner):
        return project_out(q_index, inner, w1, p_moves, [(4, HALF, 512)] * 2)

    def second_z(own, theirs):
        both = (own.astype(jnp.float32) + theirs.astype(jnp.float32)).astype(jnp.bfloat16)
        return both[0], [shift(both[at], "z", by) for by, at in ((1, 1), (-1, 3), (2, 2))]

    def second_sum(own, received, rows):
        total = rows.astype(jnp.float32) + own.astype(jnp.float32)
        for value in received:
            total = total + value.astype(jnp.float32)
        return swap(total.astype(jnp.bfloat16))

    inner_high = second_filter(p_low, p_high)
    inner_low = second_filter(tail, p_low)
    inner_high, inner_low = together(inner_high, inner_low)
    own_high, theirs_high = second_parts(inner_high)
    theirs_high = other_core(theirs_high)
    theirs_high, inner_low = together(theirs_high, inner_low)
    own_high, high_z = second_z(own_high, theirs_high)
    own_low, theirs_low = second_parts(inner_low)
    theirs_low = other_core(theirs_low)
    own_low, theirs_low, *high_z = together(own_low, theirs_low, *high_z)
    high = second_sum(own_high, high_z, high)
    own_low, low_z = second_z(own_low, theirs_low)
    low = second_sum(own_low, low_z, low)
    return jnp.concatenate([low, high], axis=0)


def solution(mesh):
    fine = Mesh(np.asarray(mesh.devices).reshape(2, 4, 2, 4, 2), AXES)
    ctx, ch = ("xl", "y", "core"), ("z", "xh")
    return jax.shard_map(
        per_device,
        mesh=fine,
        in_specs=(
            P(ctx, ch),
            P(),
            P(None, ctx, None, ch),
            P(None, None, None, ch),
            P(None, ch),
            P(None, ch),
            P(None, ch),
            P(None, ch, ctx),
        ),
        out_specs=P(ctx, ch),
        check_vma=False,
    )
```

profile of v0, /device:TPU:1, one launch (start us, length us, event | category | flops | bytes accessed | tf_op | source)
XLA Modules:
  0.0 359.2 jit_solution(13381679758839324146)
XLA Ops:
  9.9 6.0 %collective-permute-start.1 = (bf16[256,3,512]{0,2,1:T(8,128)(2,1)}, bf16[256,3,512]{0,2,1:T(8,128)(2,1)}, u32[]{:S(2)}, u32[]{:S(2)}) collective-permute-start(bf16[256,3,512]{0,2,1:T(8,128)(2,1)} %bitcast.22), channel_id=1, source_target_pairs={{1,8},{8,1},{3,10},{10,3},{5,12},{12,5},{7,14},{14,7},{17,24},{24,... | collective-permute-start | bytes 2359304 | tf_op jit(solution)/shard_map/ppermute | solution.py:24
  21.5 18.2 %collective-permute-done.1 = bf16[256,3,512]{0,2,1:T(8,128)(2,1)} collective-permute-done((bf16[256,3,512]{0,2,1:T(8,128)(2,1)}, bf16[256,3,512]{0,2,1:T(8,128)(2,1)}, u32[]{:S(2)}, u32[]{:S(2)}) %collective-permute-start.1) | collective-permute-done | bytes 786464 | tf_op jit(solution)/shard_map/ppermute | solution.py:24
  39.7 2.3 broadcast_select_fusion
  42.0 11.5 %collective-permute-done.refs_3_.refs_1_ = bf16[256,2048]{1,0:T(8,128)(2,1)S(1)} collective-permute-done((bf16[256,2048]{1,0:T(8,128)(2,1)S(1)}, bf16[256,2048]{1,0:T(8,128)(2,1)S(1)}, u32[]{:S(2)}, u32[]{:S(2)}) %collective-permute-start) | collective-permute-done | bytes 1048608 | tf_op jit(solution)/shard_map/ppermute | solution.py:20
  53.5 12.4 %collective-permute-done.4.refs_6_.refs_4_ = bf16[256,2048]{1,0:T(8,128)(2,1)} collective-permute-done((bf16[256,2048]{1,0:T(8,128)(2,1)S(1)}, bf16[256,2048]{1,0:T(8,128)(2,1)}, u32[]{:S(2)}, u32[]{:S(2)}) %collective-permute-start.4) | collective-permute-done | bytes 1048608 | tf_op jit(solution)/shard_map/ppermute | solution.py:20
  70.9 4.1 %collective-permute-start.46 = (bf16[512,256]{1,0:T(8,128)(2,1)S(1)}, bf16[512,256]{1,0:T(8,128)(2,1)S(1)}, u32[]{:S(2)}, u32[]{:S(2)}) collective-permute-start(bf16[512,256]{1,0:T(8,128)(2,1)S(1)} %slice_bitcast_fusion.11), channel_id=1, source_target_pairs={{1,8},{8,1},{3,10},{10,3},{5,12},{12,5},{7,14},{14,7},{17,24},{24,... | collective-permute-start | bytes 786440 | tf_op jit(solution)/shard_map/ppermute | solution.py:24
  75.0 8.8 %collective-permute-done.6.refs_13_.refs_11_ = bf16[256,1152]{1,0:T(8,128)(2,1)S(1)} collective-permute-done((bf16[256,1152]{1,0:T(8,128)(2,1)S(1)}, bf16[256,1152]{1,0:T(8,128)(2,1)S(1)}, u32[]{:S(2)}, u32[]{:S(2)}) %collective-permute-start.6) | collective-permute-done | bytes 589856 | tf_op jit(solution)/shard_map/ppermute | solution.py:20
  83.8 28.5 %collective-permute-done.46 = bf16[512,256]{1,0:T(8,128)(2,1)S(1)} collective-permute-done((bf16[512,256]{1,0:T(8,128)(2,1)S(1)}, bf16[512,256]{1,0:T(8,128)(2,1)S(1)}, u32[]{:S(2)}, u32[]{:S(2)}) %collective-permute-start.46) | collective-permute-done | bytes 262176 | tf_op jit(solution)/shard_map/ppermute | solution.py:24
  113.3 2.3 copy.14
  115.7 2.3 pad_maximum_fusion.2
  123.8 2.2 copy-done.2
  126.0 2.6 shard_map.82
  128.6 2.0 copy-done.15
  130.7 14.4 %shard_map.83 = (bf16[256,1536]{1,0:T(8,128)(2,1)S(1)}, bf16[256,1536]{1,0:T(8,128)(2,1)S(1)}, bf16[32,1024]{1,0:T(8,128)(2,1)S(1)}) custom-call(s32[24]{0:T(128)S(1)} %stack.120.index_ref, bf16[512,4096]{1,0:T(8,128)(2,1)} %copy-done.15, f32[512,128]{1,0:T(8,128)S(1)} %get-tuple-element.74.refs_1_, bf16[256,2048]{1,0:T(8,128)(2,1)} %copy-done, ...), custom_call_target="tpu_custom_call" | custom-call | flops 6442450944 | bytes 18874368 | tf_op jit(solution)/shard_map/pallas_call | solution.py:135
  146.4 5.2 %shard_map.85 = (bf16[256,1024]{1,0:T(8,128)(2,1)S(1)}, bf16[256,1024]{1,0:T(8,128)(2,1)}, bf16[256,1024]{1,0:T(8,128)(2,1)}, bf16[256,1024]{1,0:T(8,128)(2,1)}) custom-call(s32[24]{0:T(128)S(1)} %copy-done.12, bf16[256,1536]{1,0:T(8,128)(2,1)S(1)} %get-tuple-element.93.main_ref.before_ref, bf16[256,1536]{1,0:T(8,128)(2,1)S(1)} %get-tuple-element.100.main_ref, ...), custom_call_target="tpu_custom_call" | custom-call | flops 1073741824 | bytes 6291456 | tf_op jit(solution)/shard_map/pallas_call | solution.py:255
  151.6 3.0 collective-permute-start.25
  157.4 3.9 %collective-permute-start.19 = (bf16[32,1024]{1,0:T(8,128)(2,1)}, bf16[32,1024]{1,0:T(8,128)(2,1)S(1)}, u32[]{:S(2)}, u32[]{:S(2)}) collective-permute-start(bf16[32,1024]{1,0:T(8,128)(2,1)} %copy-done.21), channel_id=1, source_target_pairs={{0,8},{8,16},{16,24},{24,32},{32,40},{40,48},{48,56},{56,64},{64,7... | collective-permute-start | bytes 196616 | tf_op jit(solution)/shard_map/ppermute | solution.py:30
  168.2 4.5 %shard_map.84 = (bf16[256,1024]{1,0:T(8,128)(2,1)S(1)}, bf16[256,1024]{1,0:T(8,128)(2,1)S(1)}, bf16[256,1024]{1,0:T(8,128)(2,1)S(1)}, bf16[256,1024]{1,0:T(8,128)(2,1)S(1)}) custom-call(s32[24]{0:T(128)S(1)} %copy-done.13, bf16[32,1024]{1,0:T(8,128)(2,1)S(1)} %collective-permute-done.19.before_ref, ...), custom_call_target="tpu_custom_call" | custom-call | flops 1073741824 | bytes 6291456 | tf_op jit(solution)/shard_map/pallas_call | solution.py:255
  173.1 2.4 collective-permute-start.21
  175.5 2.9 collective-permute-done.24
  181.8 4.8 %collective-permute-start.27 = (bf16[256,512]{1,0:T(8,128)(2,1)S(1)}, bf16[256,512]{1,0:T(8,128)(2,1)S(1)}, u32[]{:S(2)}, u32[]{:S(2)}) collective-permute-start(bf16[256,512]{1,0:T(8,128)(2,1)S(1)} %get-tuple-element.155), channel_id=1, source_target_pairs={{1,8},{8,1},{3,10},{10,3},{5,12},{12,5},{7,14},{14,7},{17,24},{24,... | collective-permute-start | bytes 786440 | tf_op jit(solution)/shard_map/ppermute | solution.py:379
  188.0 2.2 collective-permute-done.20
  192.0 8.5 %collective-permute-done.22 = bf16[256,1024]{1,0:T(8,128)(2,1)S(1)} collective-permute-done((bf16[256,1024]{1,0:T(8,128)(2,1)S(1)}, bf16[256,1024]{1,0:T(8,128)(2,1)S(1)}, u32[]{:S(2)}, u32[]{:S(2)}) %collective-permute-start.22) | collective-permute-done | bytes 524320 | tf_op jit(solution)/shard_map/ppermute | solution.py:20
  200.5 3.5 collective-permute-done.26
  204.4 3.1 collective-permute-start.30
  208.8 4.7 %collective-permute-start.29 = (bf16[256,512]{1,0:T(8,128)(2,1)S(1)}, bf16[256,512]{1,0:T(8,128)(2,1)S(1)}, u32[]{:S(2)}, u32[]{:S(2)}) collective-permute-start(bf16[256,512]{1,0:T(8,128)(2,1)S(1)} %get-tuple-element.154), channel_id=1, source_target_pairs={{1,0},{8,9},{3,2},{10,11},{5,4},{12,13},{7,6},{14,15},{17,16},{24,... | collective-permute-start | bytes 786440 | tf_op jit(solution)/shard_map/ppermute | solution.py:378
  214.4 2.1 collective-permute-start.33
  216.5 8.4 %collective-permute-done.29 = bf16[256,512]{1,0:T(8,128)(2,1)S(1)} collective-permute-done((bf16[256,512]{1,0:T(8,128)(2,1)S(1)}, bf16[256,512]{1,0:T(8,128)(2,1)S(1)}, u32[]{:S(2)}, u32[]{:S(2)}) %collective-permute-start.29) | collective-permute-done | bytes 262176 | tf_op jit(solution)/shard_map/ppermute | solution.py:378
  224.8 2.9 collective-permute-start.34
  227.7 2.4 collective-permute-start.42
  234.5 2.4 collective-permute-start.37
  236.9 3.6 %collective-permute-start.43 = (bf16[256,512]{1,0:T(8,128)(2,1)S(1)}, bf16[256,512]{1,0:T(8,128)(2,1)S(1)}, u32[]{:S(2)}, u32[]{:S(2)}) collective-permute-start(bf16[256,512]{1,0:T(8,128)(2,1)S(1)} %collective-permute-done.32.refs_1_), channel_id=1, source_target_pairs={{0,8},{8,0},{1,9},{9,1},{2,10},{10,2},{3,11},{11,3},{4,12},{12,4},... | collective-permute-start | bytes 786440 | tf_op jit(solution)/shard_map/ppermute | solution.py:20
  240.5 8.0 %collective-permute-start.45 = (bf16[256,512]{1,0:T(8,128)(2,1)S(1)}, bf16[256,512]{1,0:T(8,128)(2,1)}, u32[]{:S(2)}, u32[]{:S(2)}) collective-permute-start(bf16[256,512]{1,0:T(8,128)(2,1)S(1)} %collective-permute-done.34.refs_3_), channel_id=1, source_target_pairs={{0,8},{8,0},{1,9},{9,1},{2,10},{10,2},{3,11},{11,3},{4,12},{12,4},... | collective-permute-start | bytes 786440 | tf_op jit(solution)/shard_map/ppermute | solution.py:20
  250.1 7.0 %collective-permute-start.47 = (f32[138,512]{1,0:T(8,128)}, f32[138,512]{1,0:T(8,128)}, u32[]{:S(2)}, u32[]{:S(2)}) collective-permute-start(f32[138,512]{1,0:T(8,128)} %pad_maximum_fusion.4), channel_id=1, source_target_pairs={{1,8},{8,1},{3,10},{10,3},{5,12},{12,5},{7,14},{14,7},{17,24},{24,... | collective-permute-start | bytes 847880 | tf_op jit(solution)/shard_map/ppermute | solution.py:24
  266.0 14.0 %shard_map.88 = (bf16[256,1536]{1,0:T(8,128)(2,1)S(1)}, bf16[256,1536]{1,0:T(8,128)(2,1)S(1)}, bf16[160,1024]{1,0:T(8,128)(2,1)S(1)}) custom-call(s32[24]{0:T(128)S(1)} %copy-done.14, bf16[256,4096]{1,0:T(8,128)(2,1)S(1)} %copy-done.18, f32[256,128]{1,0:T(8,128)S(1)} %get-tuple-element.115.refs_1_, bf16[256,4096]{1,0:T(8,128)(2,1)} %copy-done.16, ...), custom_call_target="tpu_custom_call" | custom-call | flops 6442450944 | bytes 18874368 | tf_op jit(solution)/shard_map/pallas_call | solution.py:135
  282.7 7.6 %shard_map.89.inner = bf16[256,512]{1,0:T(8,128)(2,1)S(1)} custom-call(bf16[256,1536]{1,0:T(8,128)(2,1)S(1)} %get-tuple-element.124.before_ref.main_ref, bf16[256,1536]{1,0:T(8,128)(2,1)S(1)} %get-tuple-element.125.main_ref, f32[9,512]{1,0:T(8,128)S(1)} %slice.169.feat_ref, f32[128,512]{1,0:T(8,128)S(1)} %slice.170.filter_ref, f32[1,512]{1,0:T(1,128)S(1)} %slice.171.skip_ref), custom_call_target="tpu_custom_call" | custom-call | flops 3221225472 | bytes 3145728 | tf_op jit(solution)/shard_map/pallas_call | solution.py:278
  290.3 7.6 %shard_map.90.inner = bf16[256,512]{1,0:T(8,128)(2,1)S(1)} custom-call(bf16[160,1024]{1,0:T(8,128)(2,1)S(1)} %collective-permute-done.48.before_ref, bf16[256,1536]{1,0:T(8,128)(2,1)S(1)} %get-tuple-element.124.before_ref.main_ref, f32[9,512]{1,0:T(8,128)S(1)} %slice.169.feat_ref, f32[128,512]{1,0:T(8,128)S(1)} %slice.170.filter_ref, ...), custom_call_target="tpu_custom_call" | custom-call | flops 3221225472 | bytes 3145728 | tf_op jit(solution)/shard_map/pallas_call | solution.py:278
  297.9 4.4 %shard_map.91 = (bf16[4,256,512]{2,1,0:T(8,128)(2,1)S(1)}, bf16[4,256,512]{2,1,0:T(8,128)(2,1)S(1)}) custom-call(s32[24]{0:T(128)S(1)} %copy-done.14, bf16[256,512]{1,0:T(8,128)(2,1)S(1)} %shard_map.89.inner, bf16[16,256,2048]{2,1,0:T(8,128)(2,1)} %bitcast.68), custom_call_target="tpu_custom_call" | custom-call | flops 1073741824 | bytes 6291456 | tf_op jit(solution)/shard_map/pallas_call | solution.py:301
  302.5 2.6 collective-permute-done.49
  305.1 4.4 %shard_map.92 = (bf16[4,256,512]{2,1,0:T(8,128)(2,1)S(1)}, bf16[4,256,512]{2,1,0:T(8,128)(2,1)S(1)}) custom-call(s32[24]{0:T(128)S(1)} %copy-done.14, bf16[256,512]{1,0:T(8,128)(2,1)S(1)} %shard_map.90.inner, bf16[16,256,2048]{2,1,0:T(8,128)(2,1)} %bitcast.69), custom_call_target="tpu_custom_call" | custom-call | flops 1073741824 | bytes 6291456 | tf_op jit(solution)/shard_map/pallas_call | solution.py:301
  310.4 2.7 collective-permute-start.52
  313.5 5.7 %collective-permute-done.51 = bf16[256,512]{1,0:T(8,128)(2,1)S(1)} collective-permute-done((bf16[256,512]{1,0:T(8,128)(2,1)S(1)}, bf16[256,512]{1,0:T(8,128)(2,1)S(1)}, u32[]{:S(2)}, u32[]{:S(2)}) %collective-permute-start.51) | collective-permute-done | bytes 262176 | tf_op jit(solution)/shard_map/ppermute | solution.py:20
  319.2 6.0 %collective-permute-done.53 = bf16[256,512]{1,0:T(8,128)(2,1)S(1)} collective-permute-done((bf16[256,512]{1,0:T(8,128)(2,1)S(1)}, bf16[256,512]{1,0:T(8,128)(2,1)S(1)}, u32[]{:S(2)}, u32[]{:S(2)}) %collective-permute-start.53) | collective-permute-done | bytes 262176 | tf_op jit(solution)/shard_map/ppermute | solution.py:20
  325.9 2.7 collective-permute-start.55
  328.7 7.4 %collective-permute-start.58 = (bf16[256,512]{1,0:T(8,128)(2,1)S(1)}, bf16[256,512]{1,0:T(8,128)(2,1)S(1)}, u32[]{:S(2)}, u32[]{:S(2)}) collective-permute-start(bf16[256,512]{1,0:T(8,128)(2,1)S(1)} %fusion.3), channel_id=1, source_target_pairs={{1,8},{8,1},{3,10},{10,3},{5,12},{12,5},{7,14},{14,7},{17,24},{24,... | collective-permute-start | bytes 786440 | tf_op jit(solution)/shard_map/ppermute | solution.py:24
  336.1 3.5 collective-permute-done.55
  340.5 6.4 %collective-permute-start.57 = (bf16[256,512]{1,0:T(8,128)(2,1)S(1)}, bf16[256,512]{1,0:T(8,128)(2,1)S(1)}, u32[]{:S(2)}, u32[]{:S(2)}) collective-permute-start(bf16[256,512]{1,0:T(8,128)(2,1)S(1)} %fusion.7), channel_id=1, source_target_pairs={{1,8},{8,1},{3,10},{10,3},{5,12},{12,5},{7,14},{14,7},{17,24},{24,... | collective-permute-start | bytes 786440 | tf_op jit(solution)/shard_map/ppermute | solution.py:24
  347.0 4.0 %collective-permute-done.57 = bf16[256,512]{1,0:T(8,128)(2,1)S(1)} collective-permute-done((bf16[256,512]{1,0:T(8,128)(2,1)S(1)}, bf16[256,512]{1,0:T(8,128)(2,1)S(1)}, u32[]{:S(2)}, u32[]{:S(2)}) %collective-permute-start.57) | collective-permute-done | bytes 262176 | tf_op jit(solution)/shard_map/ppermute | solution.py:24
  (198 shorter events, 62.4 us)
Async XLA Ops:
  6.5 117.2 %all-gather.5.cloned.1.call-start = ((), (), s32[]{:S(2)}) async-start(), calls=%async_computation | async-start | bytes 4718592 | tf_op jit(solution)/shard_map/all_gather | solution.py:322
  7.3 257.1 %all-gather.7.cloned.1.call-start = ((), (), s32[]{:S(2)}) async-start(), calls=%async_computation.1 | async-start | bytes 17825792 | tf_op jit(solution)/shard_map/all_gather | solution.py:318
  9.9 29.7 %collective-permute-start.1 = (bf16[256,3,512]{0,2,1:T(8,128)(2,1)}, bf16[256,3,512]{0,2,1:T(8,128)(2,1)}, u32[]{:S(2)}, u32[]{:S(2)}) collective-permute-start(bf16[256,3,512]{0,2,1:T(8,128)(2,1)} %bitcast.22), channel_id=1, source_target_pairs={{1,8},{8,1},{3,10},{10,3},{5,12},{12,5},{7,14},{14,7},{17,24},{24,... | collective-permute-start | bytes 2359304 | tf_op jit(solution)/shard_map/ppermute | solution.py:24
  16.7 36.8 %collective-permute-start = (bf16[256,2048]{1,0:T(8,128)(2,1)S(1)}, bf16[256,2048]{1,0:T(8,128)(2,1)S(1)}, u32[]{:S(2)}, u32[]{:S(2)}) collective-permute-start(bf16[256,2048]{1,0:T(8,128)(2,1)S(1)} %pad_maximum_fusion.1.refs_2_.refs_0_), channel_id=1, source_target_pairs={{0,64},{64,0},{1,65},{65,1},{2,66},{66,2},{3,67},{67,3},{4,68},{68... | collective-permute-start | bytes 3145736 | tf_op jit(solution)/shard_map/ppermute | solution.py:20
  17.1 36.4 %collective-permute-start.2 = (bf16[256,2048]{1,0:T(8,128)(2,1)S(1)}, bf16[256,2048]{1,0:T(8,128)(2,1)S(1)}, u32[]{:S(2)}, u32[]{:S(2)}) collective-permute-start(bf16[256,2048]{1,0:T(8,128)(2,1)S(1)} %pad_maximum_fusion.1.refs_2_.refs_0_), channel_id=1, source_target_pairs={{0,16},{16,32},{32,48},{48,0},{1,17},{17,33},{33,49},{49,1},{2,18}... | collective-permute-start | bytes 3145736 | tf_op jit(solution)/shard_map/ppermute | solution.py:20
  18.4 35.1 %collective-permute-start.3 = (bf16[256,2048]{1,0:T(8,128)(2,1)S(1)}, bf16[256,2048]{1,0:T(8,128)(2,1)}, u32[]{:S(2)}, u32[]{:S(2)}) collective-permute-start(bf16[256,2048]{1,0:T(8,128)(2,1)S(1)} %pad_maximum_fusion.1.refs_2_.refs_0_), channel_id=1, source_target_pairs={{0,48},{16,0},{32,16},{48,32},{1,49},{17,1},{33,17},{49,33},{2,50}... | collective-permute-start | bytes 3145736 | tf_op jit(solution)/shard_map/ppermute | solution.py:20
  19.8 46.1 %collective-permute-start.4 = (bf16[256,2048]{1,0:T(8,128)(2,1)S(1)}, bf16[256,2048]{1,0:T(8,128)(2,1)}, u32[]{:S(2)}, u32[]{:S(2)}) collective-permute-start(bf16[256,2048]{1,0:T(8,128)(2,1)S(1)} %pad_maximum_fusion.1.refs_2_.refs_0_), channel_id=1, source_target_pairs={{0,32},{16,48},{32,0},{48,16},{1,33},{17,49},{33,1},{49,17},{2,34}... | collective-permute-start | bytes 3145736 | tf_op jit(solution)/shard_map/ppermute | solution.py:20
  67.4 45.5 %collective-permute-start.5 = (bf16[3,256,896]{2,1,0:T(8,128)(2,1)S(1)}, bf16[3,256,896]{2,1,0:T(8,128)(2,1)}, u32[]{:S(2)}, u32[]{:S(2)}) collective-permute-start(bf16[3,256,896]{2,1,0:T(8,128)(2,1)S(1)} %pad_maximum_fusion), channel_id=1, source_target_pairs={{0,64},{64,0},{1,65},{65,1},{2,66},{66,2},{3,67},{67,3},{4,68},{68... | collective-permute-start | bytes 4128776 | tf_op jit(solution)/shard_map/ppermute | solution.py:20
  67.6 16.2 %collective-permute-start.6 = (bf16[256,1152]{1,0:T(8,128)(2,1)S(1)}, bf16[256,1152]{1,0:T(8,128)(2,1)S(1)}, u32[]{:S(2)}, u32[]{:S(2)}) collective-permute-start(bf16[256,1152]{1,0:T(8,128)(2,1)S(1)} %slice.137), channel_id=1, source_target_pairs={{0,16},{16,32},{32,48},{48,0},{1,17},{17,33},{33,49},{49,1},{2,18}... | collective-permute-start | bytes 1769480 | tf_op jit(solution)/shard_map/ppermute | solution.py:20
  69.1 43.2 %collective-permute-start.7 = (bf16[256,1152]{1,0:T(8,128)(2,1)S(1)}, bf16[256,1152]{1,0:T(8,128)(2,1)S(1)}, u32[]{:S(2)}, u32[]{:S(2)}) collective-permute-start(bf16[256,1152]{1,0:T(8,128)(2,1)S(1)} %slice.137), channel_id=1, source_target_pairs={{0,48},{16,0},{32,16},{48,32},{1,49},{17,1},{33,17},{49,33},{2,50}... | collective-permute-start | bytes 1769480 | tf_op jit(solution)/shard_map/ppermute | solution.py:20
  70.4 42.4 %collective-permute-start.8 = (bf16[256,1152]{1,0:T(8,128)(2,1)S(1)}, bf16[256,1152]{1,0:T(8,128)(2,1)S(1)}, u32[]{:S(2)}, u32[]{:S(2)}) collective-permute-start(bf16[256,1152]{1,0:T(8,128)(2,1)S(1)} %slice.137), channel_id=1, source_target_pairs={{0,32},{16,48},{32,0},{48,16},{1,33},{17,49},{33,1},{49,17},{2,34}... | collective-permute-start | bytes 1769480 | tf_op jit(solution)/shard_map/ppermute | solution.py:20
  70.9 41.3 %collective-permute-start.46 = (bf16[512,256]{1,0:T(8,128)(2,1)S(1)}, bf16[512,256]{1,0:T(8,128)(2,1)S(1)}, u32[]{:S(2)}, u32[]{:S(2)}) collective-permute-start(bf16[512,256]{1,0:T(8,128)(2,1)S(1)} %slice_bitcast_fusion.11), channel_id=1, source_target_pairs={{1,8},{8,1},{3,10},{10,3},{5,12},{12,5},{7,14},{14,7},{17,24},{24,... | collective-permute-start | bytes 786440 | tf_op jit(solution)/shard_map/ppermute | solution.py:24
  83.8 34.2 %collective-permute-start.9 = (bf16[256,2048]{1,0:T(8,128)(2,1)S(1)}, bf16[256,2048]{1,0:T(8,128)(2,1)}, u32[]{:S(2)}, u32[]{:S(2)}) collective-permute-start(bf16[256,2048]{1,0:T(8,128)(2,1)S(1)} %pad_maximum_fusion.1.refs_2_.refs_0_), channel_id=1, source_target_pairs={{0,8},{8,0},{1,9},{9,1},{2,10},{10,2},{3,11},{11,3},{4,12},{12,4},... | collective-permute-start | bytes 3145736 | tf_op jit(solution)/shard_map/ppermute | solution.py:20
  119.8 10.8 %collective-permute-start.14 = (bf16[3,256,896]{2,1,0:T(8,128)(2,1)}, bf16[3,256,896]{2,1,0:T(8,128)(2,1)}, u32[]{:S(2)}, u32[]{:S(2)}) collective-permute-start(bf16[3,256,896]{2,1,0:T(8,128)(2,1)} %collective-permute-done.5.refs_12_.refs_10_), channel_id=1, source_target_pairs={{0,8},{8,0},{1,9},{9,1},{2,10},{10,2},{3,11},{11,3},{4,12},{12,4},... | collective-permute-start | bytes 4128776 | tf_op jit(solution)/shard_map/ppermute | solution.py:20
  120.0 10.6 %collective-permute-start.15 = (bf16[256,1152]{1,0:T(8,128)(2,1)S(1)}, bf16[256,1152]{1,0:T(8,128)(2,1)S(1)}, u32[]{:S(2)}, u32[]{:S(2)}) collective-permute-start(bf16[256,1152]{1,0:T(8,128)(2,1)S(1)} %collective-permute-done.6.refs_13_.refs_11_), channel_id=1, source_target_pairs={{0,8},{8,0},{1,9},{9,1},{2,10},{10,2},{3,11},{11,3},{4,12},{12,4},... | collective-permute-start | bytes 1769480 | tf_op jit(solution)/shard_map/ppermute | solution.py:20
  120.4 10.2 %collective-permute-start.16 = (bf16[256,1152]{1,0:T(8,128)(2,1)S(1)}, bf16[256,1152]{1,0:T(8,128)(2,1)}, u32[]{:S(2)}, u32[]{:S(2)}) collective-permute-start(bf16[256,1152]{1,0:T(8,128)(2,1)S(1)} %collective-permute-done.7.refs_14_.refs_12_), channel_id=1, source_target_pairs={{0,8},{8,0},{1,9},{9,1},{2,10},{10,2},{3,11},{11,3},{4,12},{12,4},... | collective-permute-start | bytes 1769480 | tf_op jit(solution)/shard_map/ppermute | solution.py:20
  151.6 21.5 %collective-permute-start.25 = (bf16[256,1024]{1,0:T(8,128)(2,1)}, bf16[256,1024]{1,0:T(8,128)(2,1)}, u32[]{:S(2)}, u32[]{:S(2)}) collective-permute-start(bf16[256,1024]{1,0:T(8,128)(2,1)} %get-tuple-element.104), channel_id=1, source_target_pairs={{0,4},{2,6},{4,0},{6,2},{1,5},{3,7},{5,1},{7,3},{8,12},{10,14},{12... | collective-permute-start | bytes 1572872 | tf_op jit(solution)/shard_map/ppermute | solution.py:20
  154.5 23.9 %collective-permute-start.24 = (bf16[256,1024]{1,0:T(8,128)(2,1)}, bf16[256,1024]{1,0:T(8,128)(2,1)}, u32[]{:S(2)}, u32[]{:S(2)}) collective-permute-start(bf16[256,1024]{1,0:T(8,128)(2,1)} %get-tuple-element.103), channel_id=1, source_target_pairs={{0,6},{2,0},{4,2},{6,4},{1,7},{3,1},{5,3},{7,5},{8,14},{10,8},{12,... | collective-permute-start | bytes 1572872 | tf_op jit(solution)/shard_map/ppermute | solution.py:20
  155.3 24.7 %collective-permute-start.23 = (bf16[256,1024]{1,0:T(8,128)(2,1)}, bf16[256,1024]{1,0:T(8,128)(2,1)}, u32[]{:S(2)}, u32[]{:S(2)}) collective-permute-start(bf16[256,1024]{1,0:T(8,128)(2,1)} %get-tuple-element.102), channel_id=1, source_target_pairs={{0,2},{2,4},{4,6},{6,0},{1,3},{3,5},{5,7},{7,1},{8,10},{10,12},{12... | collective-permute-start | bytes 1572872 | tf_op jit(solution)/shard_map/ppermute | solution.py:20
  163.1 23.5 %collective-permute-start.18 = (bf16[512,512]{1,0:T(8,128)(2,1)}, bf16[512,512]{1,0:T(8,128)(2,1)S(1)}, u32[]{:S(2)}, u32[]{:S(2)}) collective-permute-start(bf16[512,512]{1,0:T(8,128)(2,1)} %param.8), channel_id=1, source_target_pairs={{1,8},{8,1},{3,10},{10,3},{5,12},{12,5},{7,14},{14,7},{17,24},{24,... | collective-permute-start | bytes 1572872 | tf_op jit(solution)/shard_map/ppermute | solution.py:24
  172.7 17.4 %collective-permute-start.20 = (bf16[256,1024]{1,0:T(8,128)(2,1)S(1)}, bf16[256,1024]{1,0:T(8,128)(2,1)S(1)}, u32[]{:S(2)}, u32[]{:S(2)}) collective-permute-start(bf16[256,1024]{1,0:T(8,128)(2,1)S(1)} %get-tuple-element.97), channel_id=1, source_target_pairs={{0,2},{2,4},{4,6},{6,0},{1,3},{3,5},{5,7},{7,1},{8,10},{10,12},{12... | collective-permute-start | bytes 1572872 | tf_op jit(solution)/shard_map/ppermute | solution.py:20
  173.1 18.9 %collective-permute-start.21 = (bf16[256,1024]{1,0:T(8,128)(2,1)S(1)}, bf16[256,1024]{1,0:T(8,128)(2,1)S(1)}, u32[]{:S(2)}, u32[]{:S(2)}) collective-permute-start(bf16[256,1024]{1,0:T(8,128)(2,1)S(1)} %get-tuple-element.98), channel_id=1, source_target_pairs={{0,6},{2,0},{4,2},{6,4},{1,7},{3,1},{5,3},{7,5},{8,14},{10,8},{12,... | collective-permute-start | bytes 1572872 | tf_op jit(solution)/shard_map/ppermute | solution.py:20
  178.4 22.0 %collective-permute-start.22 = (bf16[256,1024]{1,0:T(8,128)(2,1)S(1)}, bf16[256,1024]{1,0:T(8,128)(2,1)S(1)}, u32[]{:S(2)}, u32[]{:S(2)}) collective-permute-start(bf16[256,1024]{1,0:T(8,128)(2,1)S(1)} %get-tuple-element.99), channel_id=1, source_target_pairs={{0,4},{2,6},{4,0},{6,2},{1,5},{3,7},{5,1},{7,3},{8,12},{10,14},{12... | collective-permute-start | bytes 1572872 | tf_op jit(solution)/shard_map/ppermute | solution.py:20
  181.8 22.1 %collective-permute-start.27 = (bf16[256,512]{1,0:T(8,128)(2,1)S(1)}, bf16[256,512]{1,0:T(8,128)(2,1)S(1)}, u32[]{:S(2)}, u32[]{:S(2)}) collective-permute-start(bf16[256,512]{1,0:T(8,128)(2,1)S(1)} %get-tuple-element.155), channel_id=1, source_target_pairs={{1,8},{8,1},{3,10},{10,3},{5,12},{12,5},{7,14},{14,7},{17,24},{24,... | collective-permute-start | bytes 786440 | tf_op jit(solution)/shard_map/ppermute | solution.py:379
  186.7 17.3 %collective-permute-start.28 = (bf16[256,512]{1,0:T(8,128)(2,1)S(1)}, bf16[256,512]{1,0:T(8,128)(2,1)S(1)}, u32[]{:S(2)}, u32[]{:S(2)}) collective-permute-start(bf16[256,512]{1,0:T(8,128)(2,1)S(1)} %get-tuple-element.155), channel_id=1, source_target_pairs={{0,8},{9,1},{2,10},{11,3},{4,12},{13,5},{6,14},{15,7},{16,24},{25,... | collective-permute-start | bytes 786440 | tf_op jit(solution)/shard_map/ppermute | solution.py:380
  190.2 13.8 %collective-permute-start.26 = (bf16[256,512]{1,0:T(8,128)(2,1)S(1)}, bf16[256,512]{1,0:T(8,128)(2,1)S(1)}, u32[]{:S(2)}, u32[]{:S(2)}) collective-permute-start(bf16[256,512]{1,0:T(8,128)(2,1)S(1)} %get-tuple-element.156), channel_id=1, source_target_pairs={{1,0},{8,9},{3,2},{10,11},{5,4},{12,13},{7,6},{14,15},{17,16},{24,... | collective-permute-start | bytes 786440 | tf_op jit(solution)/shard_map/ppermute | solution.py:378
  204.4 23.4 %collective-permute-start.30 = (bf16[256,512]{1,0:T(8,128)(2,1)S(1)}, bf16[256,512]{1,0:T(8,128)(2,1)S(1)}, u32[]{:S(2)}, u32[]{:S(2)}) collective-permute-start(bf16[256,512]{1,0:T(8,128)(2,1)S(1)} %get-tuple-element.153), channel_id=1, source_target_pairs={{1,8},{8,1},{3,10},{10,3},{5,12},{12,5},{7,14},{14,7},{17,24},{24,... | collective-permute-start | bytes 786440 | tf_op jit(solution)/shard_map/ppermute | solution.py:379
  207.5 22.6 %collective-permute-start.31 = (bf16[256,512]{1,0:T(8,128)(2,1)S(1)}, bf16[256,512]{1,0:T(8,128)(2,1)S(1)}, u32[]{:S(2)}, u32[]{:S(2)}) collective-permute-start(bf16[256,512]{1,0:T(8,128)(2,1)S(1)} %get-tuple-element.153), channel_id=1, source_target_pairs={{0,8},{9,1},{2,10},{11,3},{4,12},{13,5},{6,14},{15,7},{16,24},{25,... | collective-permute-start | bytes 786440 | tf_op jit(solution)/shard_map/ppermute | solution.py:380
  208.8 16.0 %collective-permute-start.29 = (bf16[256,512]{1,0:T(8,128)(2,1)S(1)}, bf16[256,512]{1,0:T(8,128)(2,1)S(1)}, u32[]{:S(2)}, u32[]{:S(2)}) collective-permute-start(bf16[256,512]{1,0:T(8,128)(2,1)S(1)} %get-tuple-element.154), channel_id=1, source_target_pairs={{1,0},{8,9},{3,2},{10,11},{5,4},{12,13},{7,6},{14,15},{17,16},{24,... | collective-permute-start | bytes 786440 | tf_op jit(solution)/shard_map/ppermute | solution.py:378
  213.7 16.5 %collective-permute-start.32 = (bf16[256,512]{1,0:T(8,128)(2,1)S(1)}, bf16[256,512]{1,0:T(8,128)(2,1)S(1)}, u32[]{:S(2)}, u32[]{:S(2)}) collective-permute-start(bf16[256,512]{1,0:T(8,128)(2,1)S(1)} %add_convert_fusion.5.refs_0_), channel_id=1, source_target_pairs={{0,2},{2,4},{4,6},{6,0},{1,3},{3,5},{5,7},{7,1},{8,10},{10,12},{12... | collective-permute-start | bytes 786440 | tf_op jit(solution)/shard_map/ppermute | solution.py:20
  214.4 15.8 %collective-permute-start.33 = (bf16[256,512]{1,0:T(8,128)(2,1)S(1)}, bf16[256,512]{1,0:T(8,128)(2,1)S(1)}, u32[]{:S(2)}, u32[]{:S(2)}) collective-permute-start(bf16[256,512]{1,0:T(8,128)(2,1)S(1)} %add_convert_fusion.5.refs_0_), channel_id=1, source_target_pairs={{0,6},{2,0},{4,2},{6,4},{1,7},{3,1},{5,3},{7,5},{8,14},{10,8},{12,... | collective-permute-start | bytes 786440 | tf_op jit(solution)/shard_map/ppermute | solution.py:20
  227.7 12.8 %collective-permute-start.42 = (bf16[256,512]{1,0:T(8,128)(2,1)S(1)}, bf16[256,512]{1,0:T(8,128)(2,1)S(1)}, u32[]{:S(2)}, u32[]{:S(2)}) collective-permute-start(bf16[256,512]{1,0:T(8,128)(2,1)S(1)} %add_convert_fusion.5.refs_0_), channel_id=1, source_target_pairs={{0,8},{8,0},{1,9},{9,1},{2,10},{10,2},{3,11},{11,3},{4,12},{12,4},... | collective-permute-start | bytes 786440 | tf_op jit(solution)/shard_map/ppermute | solution.py:20
  233.7 14.8 %collective-permute-start.36 = (bf16[256,512]{1,0:T(8,128)(2,1)S(1)}, bf16[256,512]{1,0:T(8,128)(2,1)S(1)}, u32[]{:S(2)}, u32[]{:S(2)}) collective-permute-start(bf16[256,512]{1,0:T(8,128)(2,1)S(1)} %add_convert_fusion.4.refs_0_), channel_id=1, source_target_pairs={{0,6},{2,0},{4,2},{6,4},{1,7},{3,1},{5,3},{7,5},{8,14},{10,8},{12,... | collective-permute-start | bytes 786440 | tf_op jit(solution)/shard_map/ppermute | solution.py:20
  234.5 14.0 %collective-permute-start.37 = (bf16[256,512]{1,0:T(8,128)(2,1)S(1)}, bf16[256,512]{1,0:T(8,128)(2,1)S(1)}, u32[]{:S(2)}, u32[]{:S(2)}) collective-permute-start(bf16[256,512]{1,0:T(8,128)(2,1)S(1)} %add_convert_fusion.4.refs_0_), channel_id=1, source_target_pairs={{0,4},{2,6},{4,0},{6,2},{1,5},{3,7},{5,1},{7,3},{8,12},{10,14},{12... | collective-permute-start | bytes 786440 | tf_op jit(solution)/shard_map/ppermute | solution.py:20
  236.9 12.1 %collective-permute-start.43 = (bf16[256,512]{1,0:T(8,128)(2,1)S(1)}, bf16[256,512]{1,0:T(8,128)(2,1)S(1)}, u32[]{:S(2)}, u32[]{:S(2)}) collective-permute-start(bf16[256,512]{1,0:T(8,128)(2,1)S(1)} %collective-permute-done.32.refs_1_), channel_id=1, source_target_pairs={{0,8},{8,0},{1,9},{9,1},{2,10},{10,2},{3,11},{11,3},{4,12},{12,4},... | collective-permute-start | bytes 786440 | tf_op jit(solution)/shard_map/ppermute | solution.py:20
  248.5 12.5 %collective-permute-start.38 = (bf16[256,512]{1,0:T(8,128)(2,1)S(1)}, bf16[256,512]{1,0:T(8,128)(2,1)S(1)}, u32[]{:S(2)}, u32[]{:S(2)}) collective-permute-start(bf16[256,512]{1,0:T(8,128)(2,1)S(1)} %add_convert_fusion.4.refs_0_), channel_id=1, source_target_pairs={{0,8},{8,0},{1,9},{9,1},{2,10},{10,2},{3,11},{11,3},{4,12},{12,4},... | collective-permute-start | bytes 786440 | tf_op jit(solution)/shard_map/ppermute | solution.py:20
  248.5 12.5 %collective-permute-start.39 = (bf16[256,512]{1,0:T(8,128)(2,1)S(1)}, bf16[256,512]{1,0:T(8,128)(2,1)S(1)}, u32[]{:S(2)}, u32[]{:S(2)}) collective-permute-start(bf16[256,512]{1,0:T(8,128)(2,1)S(1)} %collective-permute-done.35.refs_1_), channel_id=1, source_target_pairs={{0,8},{8,0},{1,9},{9,1},{2,10},{10,2},{3,11},{11,3},{4,12},{12,4},... | collective-permute-start | bytes 786440 | tf_op jit(solution)/shard_map/ppermute | solution.py:20
  249.1 12.0 %collective-permute-start.40 = (bf16[256,512]{1,0:T(8,128)(2,1)S(1)}, bf16[256,512]{1,0:T(8,128)(2,1)}, u32[]{:S(2)}, u32[]{:S(2)}) collective-permute-start(bf16[256,512]{1,0:T(8,128)(2,1)S(1)} %collective-permute-done.36.refs_2_), channel_id=1, source_target_pairs={{0,8},{8,0},{1,9},{9,1},{2,10},{10,2},{3,11},{11,3},{4,12},{12,4},... | collective-permute-start | bytes 786440 | tf_op jit(solution)/shard_map/ppermute | solution.py:20
  249.1 11.9 %collective-permute-start.41 = (bf16[256,512]{1,0:T(8,128)(2,1)S(1)}, bf16[256,512]{1,0:T(8,128)(2,1)}, u32[]{:S(2)}, u32[]{:S(2)}) collective-permute-start(bf16[256,512]{1,0:T(8,128)(2,1)S(1)} %collective-permute-done.37.refs_3_), channel_id=1, source_target_pairs={{0,8},{8,0},{1,9},{9,1},{2,10},{10,2},{3,11},{11,3},{4,12},{12,4},... | collective-permute-start | bytes 786440 | tf_op jit(solution)/shard_map/ppermute | solution.py:20
  250.1 31.5 %collective-permute-start.47 = (f32[138,512]{1,0:T(8,128)}, f32[138,512]{1,0:T(8,128)}, u32[]{:S(2)}, u32[]{:S(2)}) collective-permute-start(f32[138,512]{1,0:T(8,128)} %pad_maximum_fusion.4), channel_id=1, source_target_pairs={{1,8},{8,1},{3,10},{10,3},{5,12},{12,5},{7,14},{14,7},{17,24},{24,... | collective-permute-start | bytes 847880 | tf_op jit(solution)/shard_map/ppermute | solution.py:24
  280.0 10.3 %collective-permute-start.48 = (bf16[160,1024]{1,0:T(8,128)(2,1)S(1)}, bf16[160,1024]{1,0:T(8,128)(2,1)S(1)}, u32[]{:S(2)}, u32[]{:S(2)}) collective-permute-start(bf16[160,1024]{1,0:T(8,128)(2,1)S(1)} %get-tuple-element.127), channel_id=1, source_target_pairs={{0,1},{1,16},{16,17},{17,32},{32,33},{33,48},{48,49},{49,64},{64,6... | collective-permute-start | bytes 983048 | tf_op jit(solution)/shard_map/ppermute | solution.py:30
  309.5 15.7 %collective-permute-start.50 = (bf16[4,256,512]{2,1,0:T(8,128)(2,1)S(1)}, bf16[4,256,512]{2,1,0:T(8,128)(2,1)S(1)}, u32[]{:S(2)}, u32[]{:S(2)}) collective-permute-start(bf16[4,256,512]{2,1,0:T(8,128)(2,1)S(1)} %get-tuple-element.133), channel_id=1, source_target_pairs={{0,8},{8,0},{1,9},{9,1},{2,10},{10,2},{3,11},{11,3},{4,12},{12,4},... | collective-permute-start | bytes 3145736 | tf_op jit(solution)/shard_map/ppermute | solution.py:20
  313.1 12.0 %collective-permute-start.53 = (bf16[256,512]{1,0:T(8,128)(2,1)S(1)}, bf16[256,512]{1,0:T(8,128)(2,1)S(1)}, u32[]{:S(2)}, u32[]{:S(2)}) collective-permute-start(bf16[256,512]{1,0:T(8,128)(2,1)S(1)} %get-tuple-element.150), channel_id=1, source_target_pairs={{0,4},{2,6},{4,0},{6,2},{1,5},{3,7},{5,1},{7,3},{8,12},{10,14},{12... | collective-permute-start | bytes 786440 | tf_op jit(solution)/shard_map/ppermute | solution.py:20
  325.5 10.6 %collective-permute-start.56 = (bf16[256,512]{1,0:T(8,128)(2,1)S(1)}, bf16[256,512]{1,0:T(8,128)(2,1)S(1)}, u32[]{:S(2)}, u32[]{:S(2)}) collective-permute-start(bf16[256,512]{1,0:T(8,128)(2,1)S(1)} %get-tuple-element.148), channel_id=1, source_target_pairs={{0,4},{2,6},{4,0},{6,2},{1,5},{3,7},{5,1},{7,3},{8,12},{10,14},{12... | collective-permute-start | bytes 786440 | tf_op jit(solution)/shard_map/ppermute | solution.py:20
  325.9 13.7 %collective-permute-start.55 = (bf16[256,512]{1,0:T(8,128)(2,1)S(1)}, bf16[256,512]{1,0:T(8,128)(2,1)S(1)}, u32[]{:S(2)}, u32[]{:S(2)}) collective-permute-start(bf16[256,512]{1,0:T(8,128)(2,1)S(1)} %get-tuple-element.149), channel_id=1, source_target_pairs={{0,6},{2,0},{4,2},{6,4},{1,7},{3,1},{5,3},{7,5},{8,14},{10,8},{12,... | collective-permute-start | bytes 786440 | tf_op jit(solution)/shard_map/ppermute | solution.py:20
  328.5 11.8 %collective-permute-start.54 = (bf16[256,512]{1,0:T(8,128)(2,1)S(1)}, bf16[256,512]{1,0:T(8,128)(2,1)S(1)}, u32[]{:S(2)}, u32[]{:S(2)}) collective-permute-start(bf16[256,512]{1,0:T(8,128)(2,1)S(1)} %get-tuple-element.147), channel_id=1, source_target_pairs={{0,2},{2,4},{4,6},{6,0},{1,3},{3,5},{5,7},{7,1},{8,10},{10,12},{12... | collective-permute-start | bytes 786440 | tf_op jit(solution)/shard_map/ppermute | solution.py:20
  328.7 18.2 %collective-permute-start.58 = (bf16[256,512]{1,0:T(8,128)(2,1)S(1)}, bf16[256,512]{1,0:T(8,128)(2,1)S(1)}, u32[]{:S(2)}, u32[]{:S(2)}) collective-permute-start(bf16[256,512]{1,0:T(8,128)(2,1)S(1)} %fusion.3), channel_id=1, source_target_pairs={{1,8},{8,1},{3,10},{10,3},{5,12},{12,5},{7,14},{14,7},{17,24},{24,... | collective-permute-start | bytes 786440 | tf_op jit(solution)/shard_map/ppermute | solution.py:24
  340.5 10.4 %collective-permute-start.57 = (bf16[256,512]{1,0:T(8,128)(2,1)S(1)}, bf16[256,512]{1,0:T(8,128)(2,1)S(1)}, u32[]{:S(2)}, u32[]{:S(2)}) collective-permute-start(bf16[256,512]{1,0:T(8,128)(2,1)S(1)} %fusion.7), channel_id=1, source_target_pairs={{1,8},{8,1},{3,10},{10,3},{5,12},{12,5},{7,14},{14,7},{17,24},{24,... | collective-permute-start | bytes 786440 | tf_op jit(solution)/shard_map/ppermute | solution.py:24
  (45 other events, 416.5 us)
Sparse Core Ops, SparseCore 0:
  9.7 89.2 all-gather.4
  119.9 127.4 all-gather.6
where the time goes:
time: 366 us; the launch traced here: 359 us
  waiting for transfers between devices  132 us (36%)
  starting transfers between devices  107 us (29%)
  Pallas kernels  68.7 us (19%)
  local copies, waits for them, and re-layouts  24.6 us (7%)
  between operations  14.7 us (4%)
  other arithmetic  12.3 us (3%)
    ppermute x45, waiting for transfers between devices, shift(): lax.ppermute(value, axis, [(i, (i + by) % size) for i in range(size)])  68.6 us
    ppermute x45, starting transfers between devices, shift(): lax.ppermute(value, axis, [(i, (i + by) % size) for i in range(size)])  51.9 us
    ppermute x6, waiting for transfers between devices, swap(): moved = lax.ppermute(value, ('core', 'xh'), [(1, 2), (2, 1)])  50.6 us
    ppermute x6, starting transfers between devices, swap(): moved = lax.ppermute(value, ('core', 'xh'), [(1, 2), (2, 1)])  32.8 us
    pallas_call x2, Pallas kernels, project_in(): pl.pallas_call(functools.partial(in_kernel, moves, len(rows) // 2, halo),...  28.4 us
    pallas_call x2, Pallas kernels, filtered(): pl.pallas_call(functools.partial(filter_kernel, halo, length), out_shape=...  15.2 us
    unnamed x66, local copies, waits for them, and re-layouts  15 us
    ppermute x2, waiting for transfers between devices, over_z(): lax.ppermute(mine, ('core', 'xh'), [(1, 0), (2, 3)])  11.8 us
  transfers between devices with their start and end apart: 61, of which 20 were waited for; matrix products, arithmetic and copies ran while one was open for 6% of the time, Pallas kernels for 15%

commit v1 on v0

--- a/solution.py
+++ b/solution.py
@@ -323,12 +323,14 @@
 
     m = side_by_side(in_weight[0], out_weight[0])
     m_xl = shift(m, "xl", 1)
-    m_xl, w1, *m_y = together(m_xl, swap(in_weight[1]), *[shift(m, "y", by) for by in ways])
-    o1 = swap(after(out_weight[1], m_xl))
+    m_xl, w1, o1, *m_y = together(
+        m_xl, swap(in_weight[1]), swap(after(out_weight[1], m_xl)), *[shift(m, "y", by) for by in ways]
+    )
     rest = shift(jnp.stack([v[:, CUT:] for v in m_y]), "xl", 1)
     most = [shift(m_xl[:, :CUT], "y", by) for by in ways]
-    rest, *more = together(rest, *most, *[other_core(after(v, most[0])) for v in (m, m_xl, *m_y)])
-    most, far = more[:3], more[3:]
+    rows = norm_rows(jnp.arange(8, dtype=jnp.int32), gains[0], [whole])
+    rest, *more = together(rest, *most, *rows, *[other_core(after(v, most[0])) for v in (m, m_xl, *m_y)])
+    most, rows, far = more[:3], more[3:5], more[5:]
     w_list = [m, m_xl, *m_y, *far, rest, *most] + [other_core(v) for v in (rest, *most)]
     w_moves, q_moves, slots = [], [], [z, core]
 
@@ -351,10 +353,10 @@
     q_index = jnp.stack(slots).astype(jnp.int32)
     q_list = w_list[:15]
 
-    w1 = gather(after(side_by_side(w1, o1), rest, *most), ("xh", "xl", "y"))
+    w1 = gather(after(w1.reshape(256, 1536), rest, *most), ("xh", "xl", "y"))
+    o1 = gather(o1, ("xh", "xl", "y"))
     small = jnp.concatenate([feat_filter[1].reshape(9, 512), skip_gain[1:2], mr_filter], axis=0)
 
-    rows = norm_rows(jnp.arange(8, dtype=jnp.int32), gains[0], [whole])
     low, high, tail = project_in(q_index, rows, w_list, w_moves, 16)
     base, small = after((hidden, small), low)
     base, small = swap(base), swap(small)
@@ -393,13 +395,14 @@
     *low_z, one, two, three = together(*low_z, *high_x)
     high = over_x(mine_high, (one, two, three), HALF)
     mine_low, low_x = over_z(own_low, low_z)
+    high = after(high, low_x[2])
     high_near = [shift(high, "z", by) for by in ways]
     one, two, three, *high_near = together(*low_x, *high_near)
     low = over_x(mine_low, (one, two, three), 0)
 
     places = [(p, (p // 4 % 2) * 8 + (p % 4) * 2 + p // 8) for p in range(16)]
     w_moves = [(0, p, 0, 1536, None, 0, True, block) for p, block in places]
-    p_moves = [(0, p, 1536 + 256 * half, 256, None, 256 * half, False, block) for p, block in places for half in range(2)]
+    p_moves = [(0, p, 0, 256, None, 0, False, block) for p, block in places]
     x_index = jnp.stack([behind(z, by) * 2 + c for c in (core, 1 - core) for by in (0, *ways)]).astype(jnp.int32)
 
     def normed(near):
@@ -415,7 +418,7 @@
         return filtered(before, main, small[:9], small[10:], small[9:10], 144)
 
     def second_parts(inner):
-        return project_out(q_index, inner, w1, p_moves, [(4, HALF, 512)] * 2)
+        return project_out(q_index, inner, o1, p_moves, [(4, HALF, 512)] * 2)
 
     def second_z(own, theirs):
         both = (own.astype(jnp.float32) + theirs.astype(jnp.float32)).astype(jnp.bfloat16)
@@ -432,11 +435,9 @@
     inner_high, inner_low = together(inner_high, inner_low)
     own_high, theirs_high = second_parts(inner_high)
     theirs_high = other_core(theirs_high)
-    theirs_high, inner_low = together(theirs_high, inner_low)
     own_high, high_z = second_z(own_high, theirs_high)
     own_low, theirs_low = second_parts(inner_low)
     theirs_low = other_core(theirs_low)
-    own_low, theirs_low, *high_z = together(own_low, theirs_low, *high_z)
     high = second_sum(own_high, high_z, high)
     own_low, low_z = second_z(own_low, theirs_low)
     low = second_sum(own_low, low_z, low)

time: 366 us -> 356 us (0.973)
  waiting for transfers between devices: 132 us -> 121 us
    ppermute x6, waiting for transfers between devices: 50.6 us -> 11.9 us  [swap(): moved = lax.ppermute(value, ('core', 'xh'), [(1, 2), (2, 1)])]
    ppermute x45, waiting for transfers between devices: 68.6 us -> 95 us  [shift(): lax.ppermute(value, axis, [(i, (i + by) % size) for i in range(size)])]
    ppermute x6, starting transfers between devices: 32.8 us -> 23.8 us  [swap(): moved = lax.ppermute(value, ('core', 'xh'), [(1, 2), (2, 1)])]
    ppermute x2, starting transfers between devices: 5.51 us -> 14.1 us  [from_behind(): return lax.ppermute(value, axes, [(i, i + 1) for i in range(15)])]
    ppermute x2, starting transfers between devices: 6.39 us -> 10.4 us  [over_z(): lax.ppermute(mine, ('core', 'xh'), [(1, 0), (2, 3)])]
  transfers between devices with their start and end apart: 61 -> 62, of which waited for: 20 -> 24; matrix products, arithmetic and copies ran while one was open for 6% -> 6% of each run, Pallas kernels for 15% -> 18%
where the time goes in v1:
time: 356 us; the launch traced here: 350 us
  waiting for transfers between devices  121 us (34%)
  starting transfers between devices  109 us (31%)
  Pallas kernels  68.3 us (19%)
  local copies, waits for them, and re-layouts  27.1 us (8%)
  between operations  14.1 us (4%)
  other arithmetic  10.6 us (3%)
    ppermute x45, waiting for transfers between devices, shift(): lax.ppermute(value, axis, [(i, (i + by) % size) for i in range(size)])  95 us
    ppermute x45, starting transfers between devices, shift(): lax.ppermute(value, axis, [(i, (i + by) % size) for i in range(size)])  49 us
    pallas_call x2, Pallas kernels, project_in(): pl.pallas_call(functools.partial(in_kernel, moves, len(rows) // 2, halo),...  28.8 us
    ppermute x6, starting transfers between devices, swap(): moved = lax.ppermute(value, ('core', 'xh'), [(1, 2), (2, 1)])  23.8 us
    unnamed x66, local copies, waits for them, and re-layouts  16.5 us
    pallas_call x2, Pallas kernels, filtered(): pl.pallas_call(functools.partial(filter_kernel, halo, length), out_shape=...  15.2 us
    ppermute x2, starting transfers between devices, from_behind(): return lax.ppermute(value, axes, [(i, i + 1) for i in range(15)])  14.1 us
    ppermute x2, waiting for transfers between devices, over_z(): lax.ppermute(mine, ('core', 'xh'), [(1, 0), (2, 3)])  12.5 us
  transfers between devices with their start and end apart: 62, of which 24 were waited for; matrix products, arithmetic and copies ran while one was open for 6% of the time, Pallas kernels for 18%

profile of v1, /device:TPU:1, one launch (start us, length us, event | category | flops | bytes accessed | tf_op | source)
XLA Modules:
  0.0 350.1 jit_solution(17714135750921412255)
XLA Ops:
  10.0 2.1 collective-permute-start
  13.3 5.2 %collective-permute-start.1 = (bf16[256,3,512]{0,2,1:T(8,128)(2,1)}, bf16[256,3,512]{0,2,1:T(8,128)(2,1)}, u32[]{:S(2)}, u32[]{:S(2)}) collective-permute-start(bf16[256,3,512]{0,2,1:T(8,128)(2,1)} %bitcast.21), channel_id=1, source_target_pairs={{1,8},{8,1},{3,10},{10,3},{5,12},{12,5},{7,14},{14,7},{17,24},{24,... | collective-permute-start | bytes 2359304 | tf_op jit(solution)/shard_map/ppermute | solution.py:24
  23.9 16.3 %collective-permute-done.refs_3_.refs_1_ = bf16[256,2048]{1,0:T(8,128)(2,1)S(1)} collective-permute-done((bf16[256,2048]{1,0:T(8,128)(2,1)S(1)}, bf16[256,2048]{1,0:T(8,128)(2,1)S(1)}, u32[]{:S(2)}, u32[]{:S(2)}) %collective-permute-start) | collective-permute-done | bytes 1048608 | tf_op jit(solution)/shard_map/ppermute | solution.py:20
  40.2 6.4 %collective-permute-start.2 = (bf16[512,256]{1,0:T(8,128)(2,1)S(1)}, bf16[512,256]{1,0:T(8,128)(2,1)S(1)}, u32[]{:S(2)}, u32[]{:S(2)}) collective-permute-start(bf16[512,256]{1,0:T(8,128)(2,1)S(1)} %slice_bitcast_fusion.11), channel_id=1, source_target_pairs={{1,8},{8,1},{3,10},{10,3},{5,12},{12,5},{7,14},{14,7},{17,24},{24,... | collective-permute-start | bytes 786440 | tf_op jit(solution)/shard_map/ppermute | solution.py:24
  46.6 5.8 %collective-permute-done.1 = bf16[256,3,512]{0,2,1:T(8,128)(2,1)} collective-permute-done((bf16[256,3,512]{0,2,1:T(8,128)(2,1)}, bf16[256,3,512]{0,2,1:T(8,128)(2,1)}, u32[]{:S(2)}, u32[]{:S(2)}) %collective-permute-start.1) | collective-permute-done | bytes 786464 | tf_op jit(solution)/shard_map/ppermute | solution.py:24
  52.4 2.3 broadcast_select_fusion
  56.0 10.4 %collective-permute-done.5.refs_6_.refs_4_ = bf16[256,2048]{1,0:T(8,128)(2,1)} collective-permute-done((bf16[256,2048]{1,0:T(8,128)(2,1)S(1)}, bf16[256,2048]{1,0:T(8,128)(2,1)}, u32[]{:S(2)}, u32[]{:S(2)}) %collective-permute-start.5) | collective-permute-done | bytes 1048608 | tf_op jit(solution)/shard_map/ppermute | solution.py:20
  71.4 13.0 %collective-permute-done.7.refs_13_.refs_11_ = bf16[256,1152]{1,0:T(8,128)(2,1)S(1)} collective-permute-done((bf16[256,1152]{1,0:T(8,128)(2,1)S(1)}, bf16[256,1152]{1,0:T(8,128)(2,1)S(1)}, u32[]{:S(2)}, u32[]{:S(2)}) %collective-permute-start.7) | collective-permute-done | bytes 589856 | tf_op jit(solution)/shard_map/ppermute | solution.py:20
  84.9 11.9 %collective-permute-done.9.refs_15_.refs_13_ = bf16[256,1152]{1,0:T(8,128)(2,1)S(1)} collective-permute-done((bf16[256,1152]{1,0:T(8,128)(2,1)S(1)}, bf16[256,1152]{1,0:T(8,128)(2,1)S(1)}, u32[]{:S(2)}, u32[]{:S(2)}) %collective-permute-start.9) | collective-permute-done | bytes 589856 | tf_op jit(solution)/shard_map/ppermute | solution.py:20
  96.8 11.2 %collective-permute-done.6.refs_12_.refs_10_ = bf16[3,256,896]{2,1,0:T(8,128)(2,1)} collective-permute-done((bf16[3,256,896]{2,1,0:T(8,128)(2,1)S(1)}, bf16[3,256,896]{2,1,0:T(8,128)(2,1)}, u32[]{:S(2)}, u32[]{:S(2)}) %collective-permute-start.6) | collective-permute-done | bytes 1376288 | tf_op jit(solution)/shard_map/ppermute | solution.py:20
  109.0 2.2 copy-done.2
  111.2 2.6 shard_map.82
  113.8 2.0 copy-done.16
  115.8 2.3 copy.14
  125.8 14.8 %shard_map.83 = (bf16[256,1536]{1,0:T(8,128)(2,1)S(1)}, bf16[256,1536]{1,0:T(8,128)(2,1)S(1)}, bf16[32,1024]{1,0:T(8,128)(2,1)S(1)}) custom-call(s32[24]{0:T(128)S(1)} %stack.120.index_ref, bf16[512,4096]{1,0:T(8,128)(2,1)} %copy-done.16, f32[512,128]{1,0:T(8,128)S(1)} %get-tuple-element.83.refs_1_, bf16[256,2048]{1,0:T(8,128)(2,1)} %copy-done, ...), custom_call_target="tpu_custom_call" | custom-call | flops 6442450944 | bytes 18874368 | tf_op jit(solution)/shard_map/pallas_call | solution.py:135
  141.9 5.2 %shard_map.85 = (bf16[256,1024]{1,0:T(8,128)(2,1)S(1)}, bf16[256,1024]{1,0:T(8,128)(2,1)}, bf16[256,1024]{1,0:T(8,128)(2,1)}, bf16[256,1024]{1,0:T(8,128)(2,1)}) custom-call(s32[24]{0:T(128)S(1)} %copy-done.13, bf16[256,1536]{1,0:T(8,128)(2,1)S(1)} %get-tuple-element.93.main_ref.before_ref, bf16[256,1536]{1,0:T(8,128)(2,1)S(1)} %get-tuple-element.100.main_ref, ...), custom_call_target="tpu_custom_call" | custom-call | flops 1073741824 | bytes 6291456 | tf_op jit(solution)/shard_map/pallas_call | solution.py:255
  147.2 3.0 collective-permute-start.26
  153.0 4.1 %collective-permute-start.20 = (bf16[32,1024]{1,0:T(8,128)(2,1)}, bf16[32,1024]{1,0:T(8,128)(2,1)S(1)}, u32[]{:S(2)}, u32[]{:S(2)}) collective-permute-start(bf16[32,1024]{1,0:T(8,128)(2,1)} %copy-done.22), channel_id=1, source_target_pairs={{0,8},{8,16},{16,24},{24,32},{32,40},{40,48},{48,56},{56,64},{64,7... | collective-permute-start | bytes 196616 | tf_op jit(solution)/shard_map/ppermute | solution.py:30
  158.9 2.9 collective-permute-start.19
  165.0 4.3 %shard_map.84 = (bf16[256,1024]{1,0:T(8,128)(2,1)S(1)}, bf16[256,1024]{1,0:T(8,128)(2,1)S(1)}, bf16[256,1024]{1,0:T(8,128)(2,1)S(1)}, bf16[256,1024]{1,0:T(8,128)(2,1)S(1)}) custom-call(s32[24]{0:T(128)S(1)} %copy-done.14, bf16[32,1024]{1,0:T(8,128)(2,1)S(1)} %collective-permute-done.20.before_ref, ...), custom_call_target="tpu_custom_call" | custom-call | flops 1073741824 | bytes 6291456 | tf_op jit(solution)/shard_map/pallas_call | solution.py:255
  169.8 2.4 collective-permute-start.22
  177.3 6.7 %collective-permute-start.28 = (bf16[256,512]{1,0:T(8,128)(2,1)S(1)}, bf16[256,512]{1,0:T(8,128)(2,1)S(1)}, u32[]{:S(2)}, u32[]{:S(2)}) collective-permute-start(bf16[256,512]{1,0:T(8,128)(2,1)S(1)} %get-tuple-element.149), channel_id=1, source_target_pairs={{1,8},{8,1},{3,10},{10,3},{5,12},{12,5},{7,14},{14,7},{17,24},{24,... | collective-permute-start | bytes 786440 | tf_op jit(solution)/shard_map/ppermute | solution.py:381
  185.6 5.1 %collective-permute-start.27 = (bf16[256,512]{1,0:T(8,128)(2,1)S(1)}, bf16[256,512]{1,0:T(8,128)(2,1)S(1)}, u32[]{:S(2)}, u32[]{:S(2)}) collective-permute-start(bf16[256,512]{1,0:T(8,128)(2,1)S(1)} %get-tuple-element.150), channel_id=1, source_target_pairs={{1,0},{8,9},{3,2},{10,11},{5,4},{12,13},{7,6},{14,15},{17,16},{24,... | collective-permute-start | bytes 786440 | tf_op jit(solution)/shard_map/ppermute | solution.py:380
  190.7 5.6 %collective-permute-done.23 = bf16[256,1024]{1,0:T(8,128)(2,1)S(1)} collective-permute-done((bf16[256,1024]{1,0:T(8,128)(2,1)S(1)}, bf16[256,1024]{1,0:T(8,128)(2,1)S(1)}, u32[]{:S(2)}, u32[]{:S(2)}) %collective-permute-start.23) | collective-permute-done | bytes 524320 | tf_op jit(solution)/shard_map/ppermute | solution.py:20
  196.3 4.9 %collective-permute-done.27 = bf16[256,512]{1,0:T(8,128)(2,1)S(1)} collective-permute-done((bf16[256,512]{1,0:T(8,128)(2,1)S(1)}, bf16[256,512]{1,0:T(8,128)(2,1)S(1)}, u32[]{:S(2)}, u32[]{:S(2)}) %collective-permute-start.27) | collective-permute-done | bytes 262176 | tf_op jit(solution)/shard_map/ppermute | solution.py:380
  201.7 2.5 collective-permute-start.31
  205.5 5.3 %collective-permute-start.30 = (bf16[256,512]{1,0:T(8,128)(2,1)S(1)}, bf16[256,512]{1,0:T(8,128)(2,1)S(1)}, u32[]{:S(2)}, u32[]{:S(2)}) collective-permute-start(bf16[256,512]{1,0:T(8,128)(2,1)S(1)} %get-tuple-element.148), channel_id=1, source_target_pairs={{1,0},{8,9},{3,2},{10,11},{5,4},{12,13},{7,6},{14,15},{17,16},{24,... | collective-permute-start | bytes 786440 | tf_op jit(solution)/shard_map/ppermute | solution.py:380
  213.9 7.6 %collective-permute-done.30 = bf16[256,512]{1,0:T(8,128)(2,1)S(1)} collective-permute-done((bf16[256,512]{1,0:T(8,128)(2,1)S(1)}, bf16[256,512]{1,0:T(8,128)(2,1)S(1)}, u32[]{:S(2)}, u32[]{:S(2)}) %collective-permute-start.30) | collective-permute-done | bytes 262176 | tf_op jit(solution)/shard_map/ppermute | solution.py:380
  221.5 4.1 %collective-permute-start.43 = (bf16[256,512]{1,0:T(8,128)(2,1)S(1)}, bf16[256,512]{1,0:T(8,128)(2,1)S(1)}, u32[]{:S(2)}, u32[]{:S(2)}) collective-permute-start(bf16[256,512]{1,0:T(8,128)(2,1)S(1)} %add_convert_fusion.5.refs_0_), channel_id=1, source_target_pairs={{0,8},{8,0},{1,9},{9,1},{2,10},{10,2},{3,11},{11,3},{4,12},{12,4},... | collective-permute-start | bytes 786440 | tf_op jit(solution)/shard_map/ppermute | solution.py:20
  229.6 5.6 %collective-permute-done.36.refs_1_ = bf16[256,512]{1,0:T(8,128)(2,1)S(1)} collective-permute-done((bf16[256,512]{1,0:T(8,128)(2,1)S(1)}, bf16[256,512]{1,0:T(8,128)(2,1)S(1)}, u32[]{:S(2)}, u32[]{:S(2)}) %collective-permute-start.36) | collective-permute-done | bytes 262176 | tf_op jit(solution)/shard_map/ppermute | solution.py:20
  235.2 6.2 %collective-permute-start.46 = (bf16[256,512]{1,0:T(8,128)(2,1)S(1)}, bf16[256,512]{1,0:T(8,128)(2,1)}, u32[]{:S(2)}, u32[]{:S(2)}) collective-permute-start(bf16[256,512]{1,0:T(8,128)(2,1)S(1)} %collective-permute-done.35.refs_3_), channel_id=1, source_target_pairs={{0,8},{8,0},{1,9},{9,1},{2,10},{10,2},{3,11},{11,3},{4,12},{12,4},... | collective-permute-start | bytes 786440 | tf_op jit(solution)/shard_map/ppermute | solution.py:20
  243.0 1.9 collective-permute-start.47
  248.9 2.0 shard_map.86
  253.8 14.0 %shard_map.88 = (bf16[256,1536]{1,0:T(8,128)(2,1)S(1)}, bf16[256,1536]{1,0:T(8,128)(2,1)S(1)}, bf16[160,1024]{1,0:T(8,128)(2,1)S(1)}) custom-call(s32[24]{0:T(128)S(1)} %copy-done.15, bf16[256,4096]{1,0:T(8,128)(2,1)S(1)} %copy-done.19, f32[256,128]{1,0:T(8,128)S(1)} %get-tuple-element.116.refs_1_, bf16[256,4096]{1,0:T(8,128)(2,1)} %copy-done.17, ...), custom_call_target="tpu_custom_call" | custom-call | flops 6442450944 | bytes 18874368 | tf_op jit(solution)/shard_map/pallas_call | solution.py:135
  267.8 10.0 %collective-permute-start.48 = (bf16[160,1024]{1,0:T(8,128)(2,1)S(1)}, bf16[160,1024]{1,0:T(8,128)(2,1)S(1)}, u32[]{:S(2)}, u32[]{:S(2)}) collective-permute-start(bf16[160,1024]{1,0:T(8,128)(2,1)S(1)} %get-tuple-element.127), channel_id=1, source_target_pairs={{0,1},{1,16},{16,17},{17,32},{32,33},{33,48},{48,49},{49,64},{64,6... | collective-permute-start | bytes 983048 | tf_op jit(solution)/shard_map/ppermute | solution.py:30
  278.9 7.6 %shard_map.89.inner = bf16[256,512]{1,0:T(8,128)(2,1)S(1)} custom-call(bf16[256,1536]{1,0:T(8,128)(2,1)S(1)} %get-tuple-element.124.before_ref.main_ref, bf16[256,1536]{1,0:T(8,128)(2,1)S(1)} %get-tuple-element.125.main_ref, f32[9,512]{1,0:T(8,128)S(1)} %slice.159.feat_ref, f32[128,512]{1,0:T(8,128)S(1)} %slice.160.filter_ref, f32[1,512]{1,0:T(1,128)S(1)} %slice.161.skip_ref), custom_call_target="tpu_custom_call" | custom-call | flops 3221225472 | bytes 3145728 | tf_op jit(solution)/shard_map/pallas_call | solution.py:278
  286.6 7.6 %shard_map.90.inner = bf16[256,512]{1,0:T(8,128)(2,1)S(1)} custom-call(bf16[160,1024]{1,0:T(8,128)(2,1)S(1)} %collective-permute-done.48.before_ref, bf16[256,1536]{1,0:T(8,128)(2,1)S(1)} %get-tuple-element.124.before_ref.main_ref, f32[9,512]{1,0:T(8,128)S(1)} %slice.159.feat_ref, f32[128,512]{1,0:T(8,128)S(1)} %slice.160.filter_ref, ...), custom_call_target="tpu_custom_call" | custom-call | flops 3221225472 | bytes 3145728 | tf_op jit(solution)/shard_map/pallas_call | solution.py:278
  294.2 4.1 %shard_map.92 = (bf16[4,256,512]{2,1,0:T(8,128)(2,1)S(1)}, bf16[4,256,512]{2,1,0:T(8,128)(2,1)S(1)}) custom-call(s32[24]{0:T(128)S(1)} %copy-done.15, bf16[256,512]{1,0:T(8,128)(2,1)S(1)} %shard_map.89.inner, bf16[16,512,256]{2,1,0:T(8,128)(2,1)} %bitcast.68), custom_call_target="tpu_custom_call" | custom-call | flops 1073741824 | bytes 6291456 | tf_op jit(solution)/shard_map/pallas_call | solution.py:301
  298.3 3.4 collective-permute-start.54
  301.7 4.1 %shard_map.91 = (bf16[4,256,512]{2,1,0:T(8,128)(2,1)S(1)}, bf16[4,256,512]{2,1,0:T(8,128)(2,1)S(1)}) custom-call(s32[24]{0:T(128)S(1)} %copy-done.15, bf16[256,512]{1,0:T(8,128)(2,1)S(1)} %shard_map.90.inner, bf16[16,512,256]{2,1,0:T(8,128)(2,1)} %bitcast.69), custom_call_target="tpu_custom_call" | custom-call | flops 1073741824 | bytes 6291456 | tf_op jit(solution)/shard_map/pallas_call | solution.py:301
  309.3 2.1 collective-permute-start.52
  313.2 2.2 collective-permute-done.57
  315.5 5.0 %collective-permute-done.56 = bf16[256,512]{1,0:T(8,128)(2,1)S(1)} collective-permute-done((bf16[256,512]{1,0:T(8,128)(2,1)S(1)}, bf16[256,512]{1,0:T(8,128)(2,1)S(1)}, u32[]{:S(2)}, u32[]{:S(2)}) %collective-permute-start.56) | collective-permute-done | bytes 262176 | tf_op jit(solution)/shard_map/ppermute | solution.py:20
  320.5 2.2 collective-permute-done.55
  322.8 3.8 %collective-permute-start.58 = (bf16[256,512]{1,0:T(8,128)(2,1)S(1)}, bf16[256,512]{1,0:T(8,128)(2,1)S(1)}, u32[]{:S(2)}, u32[]{:S(2)}) collective-permute-start(bf16[256,512]{1,0:T(8,128)(2,1)S(1)} %fusion.3), channel_id=1, source_target_pairs={{1,8},{8,1},{3,10},{10,3},{5,12},{12,5},{7,14},{14,7},{17,24},{24,... | collective-permute-start | bytes 786440 | tf_op jit(solution)/shard_map/ppermute | solution.py:24
  326.7 5.0 %collective-permute-done.51 = bf16[256,512]{1,0:T(8,128)(2,1)S(1)} collective-permute-done((bf16[256,512]{1,0:T(8,128)(2,1)S(1)}, bf16[256,512]{1,0:T(8,128)(2,1)S(1)}, u32[]{:S(2)}, u32[]{:S(2)}) %collective-permute-start.51) | collective-permute-done | bytes 262176 | tf_op jit(solution)/shard_map/ppermute | solution.py:20
  333.3 3.5 %collective-permute-start.53 = (bf16[256,512]{1,0:T(8,128)(2,1)S(1)}, bf16[256,512]{1,0:T(8,128)(2,1)S(1)}, u32[]{:S(2)}, u32[]{:S(2)}) collective-permute-start(bf16[256,512]{1,0:T(8,128)(2,1)S(1)} %fusion.7), channel_id=1, source_target_pairs={{1,8},{8,1},{3,10},{10,3},{5,12},{12,5},{7,14},{14,7},{17,24},{24,... | collective-permute-start | bytes 786440 | tf_op jit(solution)/shard_map/ppermute | solution.py:24
  336.9 5.6 %collective-permute-done.53 = bf16[256,512]{1,0:T(8,128)(2,1)S(1)} collective-permute-done((bf16[256,512]{1,0:T(8,128)(2,1)S(1)}, bf16[256,512]{1,0:T(8,128)(2,1)S(1)}, u32[]{:S(2)}, u32[]{:S(2)}) %collective-permute-start.53) | collective-permute-done | bytes 262176 | tf_op jit(solution)/shard_map/ppermute | solution.py:24
  (199 shorter events, 67.6 us)
Async XLA Ops:
  6.5 102.4 %all-gather.7.cloned.1.call-start = ((), (), s32[]{:S(2)}) async-start(), calls=%async_computation | async-start | bytes 4718592 | tf_op jit(solution)/shard_map/all_gather | solution.py:322
  7.3 244.9 %all-gather.9.cloned.1.call-start = ((), (), s32[]{:S(2)}) async-start(), calls=%async_computation.1 | async-start | bytes 13369344 | tf_op jit(solution)/shard_map/all_gather | solution.py:318
  10.0 30.2 %collective-permute-start = (bf16[256,2048]{1,0:T(8,128)(2,1)S(1)}, bf16[256,2048]{1,0:T(8,128)(2,1)S(1)}, u32[]{:S(2)}, u32[]{:S(2)}) collective-permute-start(bf16[256,2048]{1,0:T(8,128)(2,1)S(1)} %pad_maximum_fusion.1.refs_2_.refs_0_), channel_id=1, source_target_pairs={{0,64},{64,0},{1,65},{65,1},{2,66},{66,2},{3,67},{67,3},{4,68},{68... | collective-permute-start | bytes 3145736 | tf_op jit(solution)/shard_map/ppermute | solution.py:20
  13.3 39.2 %collective-permute-start.1 = (bf16[256,3,512]{0,2,1:T(8,128)(2,1)}, bf16[256,3,512]{0,2,1:T(8,128)(2,1)}, u32[]{:S(2)}, u32[]{:S(2)}) collective-permute-start(bf16[256,3,512]{0,2,1:T(8,128)(2,1)} %bitcast.21), channel_id=1, source_target_pairs={{1,8},{8,1},{3,10},{10,3},{5,12},{12,5},{7,14},{14,7},{17,24},{24,... | collective-permute-start | bytes 2359304 | tf_op jit(solution)/shard_map/ppermute | solution.py:24
  18.4 37.5 %collective-permute-start.3 = (bf16[256,2048]{1,0:T(8,128)(2,1)S(1)}, bf16[256,2048]{1,0:T(8,128)(2,1)S(1)}, u32[]{:S(2)}, u32[]{:S(2)}) collective-permute-start(bf16[256,2048]{1,0:T(8,128)(2,1)S(1)} %pad_maximum_fusion.1.refs_2_.refs_0_), channel_id=1, source_target_pairs={{0,16},{16,32},{32,48},{48,0},{1,17},{17,33},{33,49},{49,1},{2,18}... | collective-permute-start | bytes 3145736 | tf_op jit(solution)/shard_map/ppermute | solution.py:20
  19.8 36.2 %collective-permute-start.4 = (bf16[256,2048]{1,0:T(8,128)(2,1)S(1)}, bf16[256,2048]{1,0:T(8,128)(2,1)}, u32[]{:S(2)}, u32[]{:S(2)}) collective-permute-start(bf16[256,2048]{1,0:T(8,128)(2,1)S(1)} %pad_maximum_fusion.1.refs_2_.refs_0_), channel_id=1, source_target_pairs={{0,48},{16,0},{32,16},{48,32},{1,49},{17,1},{33,17},{49,33},{2,50}... | collective-permute-start | bytes 3145736 | tf_op jit(solution)/shard_map/ppermute | solution.py:20
  21.3 45.1 %collective-permute-start.5 = (bf16[256,2048]{1,0:T(8,128)(2,1)S(1)}, bf16[256,2048]{1,0:T(8,128)(2,1)}, u32[]{:S(2)}, u32[]{:S(2)}) collective-permute-start(bf16[256,2048]{1,0:T(8,128)(2,1)S(1)} %pad_maximum_fusion.1.refs_2_.refs_0_), channel_id=1, source_target_pairs={{0,32},{16,48},{32,0},{48,16},{1,33},{17,49},{33,1},{49,17},{2,34}... | collective-permute-start | bytes 3145736 | tf_op jit(solution)/shard_map/ppermute | solution.py:20
  40.2 15.0 %collective-permute-start.2 = (bf16[512,256]{1,0:T(8,128)(2,1)S(1)}, bf16[512,256]{1,0:T(8,128)(2,1)S(1)}, u32[]{:S(2)}, u32[]{:S(2)}) collective-permute-start(bf16[512,256]{1,0:T(8,128)(2,1)S(1)} %slice_bitcast_fusion.11), channel_id=1, source_target_pairs={{1,8},{8,1},{3,10},{10,3},{5,12},{12,5},{7,14},{14,7},{17,24},{24,... | collective-permute-start | bytes 786440 | tf_op jit(solution)/shard_map/ppermute | solution.py:24
  67.9 40.2 %collective-permute-start.6 = (bf16[3,256,896]{2,1,0:T(8,128)(2,1)S(1)}, bf16[3,256,896]{2,1,0:T(8,128)(2,1)}, u32[]{:S(2)}, u32[]{:S(2)}) collective-permute-start(bf16[3,256,896]{2,1,0:T(8,128)(2,1)S(1)} %pad_maximum_fusion), channel_id=1, source_target_pairs={{0,64},{64,0},{1,65},{65,1},{2,66},{66,2},{3,67},{67,3},{4,68},{68... | collective-permute-start | bytes 4128776 | tf_op jit(solution)/shard_map/ppermute | solution.py:20
  68.1 16.3 %collective-permute-start.7 = (bf16[256,1152]{1,0:T(8,128)(2,1)S(1)}, bf16[256,1152]{1,0:T(8,128)(2,1)S(1)}, u32[]{:S(2)}, u32[]{:S(2)}) collective-permute-start(bf16[256,1152]{1,0:T(8,128)(2,1)S(1)} %slice.131), channel_id=1, source_target_pairs={{0,16},{16,32},{32,48},{48,0},{1,17},{17,33},{33,49},{49,1},{2,18}... | collective-permute-start | bytes 1769480 | tf_op jit(solution)/shard_map/ppermute | solution.py:20
  69.5 15.4 %collective-permute-start.8 = (bf16[256,1152]{1,0:T(8,128)(2,1)S(1)}, bf16[256,1152]{1,0:T(8,128)(2,1)S(1)}, u32[]{:S(2)}, u32[]{:S(2)}) collective-permute-start(bf16[256,1152]{1,0:T(8,128)(2,1)S(1)} %slice.131), channel_id=1, source_target_pairs={{0,48},{16,0},{32,16},{48,32},{1,49},{17,1},{33,17},{49,33},{2,50}... | collective-permute-start | bytes 1769480 | tf_op jit(solution)/shard_map/ppermute | solution.py:20
  70.8 26.0 %collective-permute-start.9 = (bf16[256,1152]{1,0:T(8,128)(2,1)S(1)}, bf16[256,1152]{1,0:T(8,128)(2,1)S(1)}, u32[]{:S(2)}, u32[]{:S(2)}) collective-permute-start(bf16[256,1152]{1,0:T(8,128)(2,1)S(1)} %slice.131), channel_id=1, source_target_pairs={{0,32},{16,48},{32,0},{48,16},{1,33},{17,49},{33,1},{49,17},{2,34}... | collective-permute-start | bytes 1769480 | tf_op jit(solution)/shard_map/ppermute | solution.py:20
  84.3 31.5 %collective-permute-start.10 = (bf16[256,2048]{1,0:T(8,128)(2,1)S(1)}, bf16[256,2048]{1,0:T(8,128)(2,1)}, u32[]{:S(2)}, u32[]{:S(2)}) collective-permute-start(bf16[256,2048]{1,0:T(8,128)(2,1)S(1)} %pad_maximum_fusion.1.refs_2_.refs_0_), channel_id=1, source_target_pairs={{0,8},{8,0},{1,9},{9,1},{2,10},{10,2},{3,11},{11,3},{4,12},{12,4},... | collective-permute-start | bytes 3145736 | tf_op jit(solution)/shard_map/ppermute | solution.py:20
  84.4 31.5 %collective-permute-start.11 = (bf16[256,2048]{1,0:T(8,128)(2,1)}, bf16[256,2048]{1,0:T(8,128)(2,1)}, u32[]{:S(2)}, u32[]{:S(2)}) collective-permute-start(bf16[256,2048]{1,0:T(8,128)(2,1)} %copy-done.23), channel_id=1, source_target_pairs={{0,8},{8,0},{1,9},{9,1},{2,10},{10,2},{3,11},{11,3},{4,12},{12,4},... | collective-permute-start | bytes 3145736 | tf_op jit(solution)/shard_map/ppermute | solution.py:20
  84.9 30.9 %collective-permute-start.12 = (bf16[256,2048]{1,0:T(8,128)(2,1)}, bf16[256,2048]{1,0:T(8,128)(2,1)}, u32[]{:S(2)}, u32[]{:S(2)}) collective-permute-start(bf16[256,2048]{1,0:T(8,128)(2,1)} %copy-done.24), channel_id=1, source_target_pairs={{0,8},{8,0},{1,9},{9,1},{2,10},{10,2},{3,11},{11,3},{4,12},{12,4},... | collective-permute-start | bytes 3145736 | tf_op jit(solution)/shard_map/ppermute | solution.py:20
  96.8 19.0 %collective-permute-start.13 = (bf16[256,2048]{1,0:T(8,128)(2,1)}, bf16[256,2048]{1,0:T(8,128)(2,1)}, u32[]{:S(2)}, u32[]{:S(2)}) collective-permute-start(bf16[256,2048]{1,0:T(8,128)(2,1)} %collective-permute-done.4.refs_5_.refs_3_), channel_id=1, source_target_pairs={{0,8},{8,0},{1,9},{9,1},{2,10},{10,2},{3,11},{11,3},{4,12},{12,4},... | collective-permute-start | bytes 3145736 | tf_op jit(solution)/shard_map/ppermute | solution.py:20
  118.2 176.0 %all-gather.11.cloned.1.call-start = ((), (), s32[]{:S(2)}) async-start(), calls=%async_computation.2 | async-start | bytes 4456448 | tf_op jit(solution)/shard_map/all_gather | solution.py:318
  147.2 22.6 %collective-permute-start.26 = (bf16[256,1024]{1,0:T(8,128)(2,1)}, bf16[256,1024]{1,0:T(8,128)(2,1)}, u32[]{:S(2)}, u32[]{:S(2)}) collective-permute-start(bf16[256,1024]{1,0:T(8,128)(2,1)} %get-tuple-element.104), channel_id=1, source_target_pairs={{0,4},{2,6},{4,0},{6,2},{1,5},{3,7},{5,1},{7,3},{8,12},{10,14},{12... | collective-permute-start | bytes 1572872 | tf_op jit(solution)/shard_map/ppermute | solution.py:20
  150.2 23.6 %collective-permute-start.25 = (bf16[256,1024]{1,0:T(8,128)(2,1)}, bf16[256,1024]{1,0:T(8,128)(2,1)}, u32[]{:S(2)}, u32[]{:S(2)}) collective-permute-start(bf16[256,1024]{1,0:T(8,128)(2,1)} %get-tuple-element.103), channel_id=1, source_target_pairs={{0,6},{2,0},{4,2},{6,4},{1,7},{3,1},{5,3},{7,5},{8,14},{10,8},{12,... | collective-permute-start | bytes 1572872 | tf_op jit(solution)/shard_map/ppermute | solution.py:20
  151.0 24.5 %collective-permute-start.24 = (bf16[256,1024]{1,0:T(8,128)(2,1)}, bf16[256,1024]{1,0:T(8,128)(2,1)}, u32[]{:S(2)}, u32[]{:S(2)}) collective-permute-start(bf16[256,1024]{1,0:T(8,128)(2,1)} %get-tuple-element.102), channel_id=1, source_target_pairs={{0,2},{2,4},{4,6},{6,0},{1,3},{3,5},{5,7},{7,1},{8,10},{10,12},{12... | collective-permute-start | bytes 1572872 | tf_op jit(solution)/shard_map/ppermute | solution.py:20
  153.0 8.8 %collective-permute-start.20 = (bf16[32,1024]{1,0:T(8,128)(2,1)}, bf16[32,1024]{1,0:T(8,128)(2,1)S(1)}, u32[]{:S(2)}, u32[]{:S(2)}) collective-permute-start(bf16[32,1024]{1,0:T(8,128)(2,1)} %copy-done.22), channel_id=1, source_target_pairs={{0,8},{8,16},{16,24},{24,32},{32,40},{40,48},{48,56},{56,64},{64,7... | collective-permute-start | bytes 196616 | tf_op jit(solution)/shard_map/ppermute | solution.py:30
  158.9 25.1 %collective-permute-start.19 = (bf16[512,512]{1,0:T(8,128)(2,1)}, bf16[512,512]{1,0:T(8,128)(2,1)S(1)}, u32[]{:S(2)}, u32[]{:S(2)}) collective-permute-start(bf16[512,512]{1,0:T(8,128)(2,1)} %param.8), channel_id=1, source_target_pairs={{1,8},{8,1},{3,10},{10,3},{5,12},{12,5},{7,14},{14,7},{17,24},{24,... | collective-permute-start | bytes 1572872 | tf_op jit(solution)/shard_map/ppermute | solution.py:24
  169.4 16.2 %collective-permute-start.21 = (bf16[256,1024]{1,0:T(8,128)(2,1)S(1)}, bf16[256,1024]{1,0:T(8,128)(2,1)S(1)}, u32[]{:S(2)}, u32[]{:S(2)}) collective-permute-start(bf16[256,1024]{1,0:T(8,128)(2,1)S(1)} %get-tuple-element.97), channel_id=1, source_target_pairs={{0,2},{2,4},{4,6},{6,0},{1,3},{3,5},{5,7},{7,1},{8,10},{10,12},{12... | collective-permute-start | bytes 1572872 | tf_op jit(solution)/shard_map/ppermute | solution.py:20
  169.8 21.0 %collective-permute-start.22 = (bf16[256,1024]{1,0:T(8,128)(2,1)S(1)}, bf16[256,1024]{1,0:T(8,128)(2,1)S(1)}, u32[]{:S(2)}, u32[]{:S(2)}) collective-permute-start(bf16[256,1024]{1,0:T(8,128)(2,1)S(1)} %get-tuple-element.98), channel_id=1, source_target_pairs={{0,6},{2,0},{4,2},{6,4},{1,7},{3,1},{5,3},{7,5},{8,14},{10,8},{12,... | collective-permute-start | bytes 1572872 | tf_op jit(solution)/shard_map/ppermute | solution.py:20
  173.8 22.5 %collective-permute-start.23 = (bf16[256,1024]{1,0:T(8,128)(2,1)S(1)}, bf16[256,1024]{1,0:T(8,128)(2,1)S(1)}, u32[]{:S(2)}, u32[]{:S(2)}) collective-permute-start(bf16[256,1024]{1,0:T(8,128)(2,1)S(1)} %get-tuple-element.99), channel_id=1, source_target_pairs={{0,4},{2,6},{4,0},{6,2},{1,5},{3,7},{5,1},{7,3},{8,12},{10,14},{12... | collective-permute-start | bytes 1572872 | tf_op jit(solution)/shard_map/ppermute | solution.py:20
  177.3 24.0 %collective-permute-start.28 = (bf16[256,512]{1,0:T(8,128)(2,1)S(1)}, bf16[256,512]{1,0:T(8,128)(2,1)S(1)}, u32[]{:S(2)}, u32[]{:S(2)}) collective-permute-start(bf16[256,512]{1,0:T(8,128)(2,1)S(1)} %get-tuple-element.149), channel_id=1, source_target_pairs={{1,8},{8,1},{3,10},{10,3},{5,12},{12,5},{7,14},{14,7},{17,24},{24,... | collective-permute-start | bytes 786440 | tf_op jit(solution)/shard_map/ppermute | solution.py:381
  183.9 17.3 %collective-permute-start.29 = (bf16[256,512]{1,0:T(8,128)(2,1)S(1)}, bf16[256,512]{1,0:T(8,128)(2,1)S(1)}, u32[]{:S(2)}, u32[]{:S(2)}) collective-permute-start(bf16[256,512]{1,0:T(8,128)(2,1)S(1)} %get-tuple-element.149), channel_id=1, source_target_pairs={{0,8},{9,1},{2,10},{11,3},{4,12},{13,5},{6,14},{15,7},{16,24},{25,... | collective-permute-start | bytes 786440 | tf_op jit(solution)/shard_map/ppermute | solution.py:382
  185.6 15.7 %collective-permute-start.27 = (bf16[256,512]{1,0:T(8,128)(2,1)S(1)}, bf16[256,512]{1,0:T(8,128)(2,1)S(1)}, u32[]{:S(2)}, u32[]{:S(2)}) collective-permute-start(bf16[256,512]{1,0:T(8,128)(2,1)S(1)} %get-tuple-element.150), channel_id=1, source_target_pairs={{1,0},{8,9},{3,2},{10,11},{5,4},{12,13},{7,6},{14,15},{17,16},{24,... | collective-permute-start | bytes 786440 | tf_op jit(solution)/shard_map/ppermute | solution.py:380
  201.7 23.9 %collective-permute-start.31 = (bf16[256,512]{1,0:T(8,128)(2,1)S(1)}, bf16[256,512]{1,0:T(8,128)(2,1)S(1)}, u32[]{:S(2)}, u32[]{:S(2)}) collective-permute-start(bf16[256,512]{1,0:T(8,128)(2,1)S(1)} %get-tuple-element.147), channel_id=1, source_target_pairs={{1,8},{8,1},{3,10},{10,3},{5,12},{12,5},{7,14},{14,7},{17,24},{24,... | collective-permute-start | bytes 786440 | tf_op jit(solution)/shard_map/ppermute | solution.py:381
  205.5 16.0 %collective-permute-start.30 = (bf16[256,512]{1,0:T(8,128)(2,1)S(1)}, bf16[256,512]{1,0:T(8,128)(2,1)S(1)}, u32[]{:S(2)}, u32[]{:S(2)}) collective-permute-start(bf16[256,512]{1,0:T(8,128)(2,1)S(1)} %get-tuple-element.148), channel_id=1, source_target_pairs={{1,0},{8,9},{3,2},{10,11},{5,4},{12,13},{7,6},{14,15},{17,16},{24,... | collective-permute-start | bytes 786440 | tf_op jit(solution)/shard_map/ppermute | solution.py:380
  211.0 14.6 %collective-permute-start.33 = (bf16[256,512]{1,0:T(8,128)(2,1)S(1)}, bf16[256,512]{1,0:T(8,128)(2,1)S(1)}, u32[]{:S(2)}, u32[]{:S(2)}) collective-permute-start(bf16[256,512]{1,0:T(8,128)(2,1)S(1)} %add_convert_fusion.5.refs_0_), channel_id=1, source_target_pairs={{0,2},{2,4},{4,6},{6,0},{1,3},{3,5},{5,7},{7,1},{8,10},{10,12},{12... | collective-permute-start | bytes 786440 | tf_op jit(solution)/shard_map/ppermute | solution.py:20
  211.9 13.7 %collective-permute-start.34 = (bf16[256,512]{1,0:T(8,128)(2,1)S(1)}, bf16[256,512]{1,0:T(8,128)(2,1)S(1)}, u32[]{:S(2)}, u32[]{:S(2)}) collective-permute-start(bf16[256,512]{1,0:T(8,128)(2,1)S(1)} %add_convert_fusion.5.refs_0_), channel_id=1, source_target_pairs={{0,6},{2,0},{4,2},{6,4},{1,7},{3,1},{5,3},{7,5},{8,14},{10,8},{12,... | collective-permute-start | bytes 786440 | tf_op jit(solution)/shard_map/ppermute | solution.py:20
  213.8 11.8 %collective-permute-start.35 = (bf16[256,512]{1,0:T(8,128)(2,1)S(1)}, bf16[256,512]{1,0:T(8,128)(2,1)S(1)}, u32[]{:S(2)}, u32[]{:S(2)}) collective-permute-start(bf16[256,512]{1,0:T(8,128)(2,1)S(1)} %add_convert_fusion.5.refs_0_), channel_id=1, source_target_pairs={{0,4},{2,6},{4,0},{6,2},{1,5},{3,7},{5,1},{7,3},{8,12},{10,14},{12... | collective-permute-start | bytes 786440 | tf_op jit(solution)/shard_map/ppermute | solution.py:20
  225.8 9.4 %collective-permute-start.36 = (bf16[256,512]{1,0:T(8,128)(2,1)S(1)}, bf16[256,512]{1,0:T(8,128)(2,1)S(1)}, u32[]{:S(2)}, u32[]{:S(2)}) collective-permute-start(bf16[256,512]{1,0:T(8,128)(2,1)S(1)} %add_convert_fusion.4.refs_0_), channel_id=1, source_target_pairs={{0,2},{2,4},{4,6},{6,0},{1,3},{3,5},{5,7},{7,1},{8,10},{10,12},{12... | collective-permute-start | bytes 786440 | tf_op jit(solution)/shard_map/ppermute | solution.py:20
  226.7 14.7 %collective-permute-start.37 = (bf16[256,512]{1,0:T(8,128)(2,1)S(1)}, bf16[256,512]{1,0:T(8,128)(2,1)S(1)}, u32[]{:S(2)}, u32[]{:S(2)}) collective-permute-start(bf16[256,512]{1,0:T(8,128)(2,1)S(1)} %add_convert_fusion.4.refs_0_), channel_id=1, source_target_pairs={{0,6},{2,0},{4,2},{6,4},{1,7},{3,1},{5,3},{7,5},{8,14},{10,8},{12,... | collective-permute-start | bytes 786440 | tf_op jit(solution)/shard_map/ppermute | solution.py:20
  228.5 12.9 %collective-permute-start.38 = (bf16[256,512]{1,0:T(8,128)(2,1)S(1)}, bf16[256,512]{1,0:T(8,128)(2,1)S(1)}, u32[]{:S(2)}, u32[]{:S(2)}) collective-permute-start(bf16[256,512]{1,0:T(8,128)(2,1)S(1)} %add_convert_fusion.4.refs_0_), channel_id=1, source_target_pairs={{0,4},{2,6},{4,0},{6,2},{1,5},{3,7},{5,1},{7,3},{8,12},{10,14},{12... | collective-permute-start | bytes 786440 | tf_op jit(solution)/shard_map/ppermute | solution.py:20
  228.7 13.2 %collective-permute-start.44 = (bf16[256,512]{1,0:T(8,128)(2,1)S(1)}, bf16[256,512]{1,0:T(8,128)(2,1)S(1)}, u32[]{:S(2)}, u32[]{:S(2)}) collective-permute-start(bf16[256,512]{1,0:T(8,128)(2,1)S(1)} %collective-permute-done.33.refs_1_), channel_id=1, source_target_pairs={{0,8},{8,0},{1,9},{9,1},{2,10},{10,2},{3,11},{11,3},{4,12},{12,4},... | collective-permute-start | bytes 786440 | tf_op jit(solution)/shard_map/ppermute | solution.py:20
  229.6 12.5 %collective-permute-start.45 = (bf16[256,512]{1,0:T(8,128)(2,1)S(1)}, bf16[256,512]{1,0:T(8,128)(2,1)S(1)}, u32[]{:S(2)}, u32[]{:S(2)}) collective-permute-start(bf16[256,512]{1,0:T(8,128)(2,1)S(1)} %collective-permute-done.34.refs_2_), channel_id=1, source_target_pairs={{0,8},{8,0},{1,9},{9,1},{2,10},{10,2},{3,11},{11,3},{4,12},{12,4},... | collective-permute-start | bytes 786440 | tf_op jit(solution)/shard_map/ppermute | solution.py:20
  243.0 34.8 %collective-permute-start.47 = (f32[138,512]{1,0:T(8,128)}, f32[138,512]{1,0:T(8,128)}, u32[]{:S(2)}, u32[]{:S(2)}) collective-permute-start(f32[138,512]{1,0:T(8,128)} %pad_maximum_fusion.3), channel_id=1, source_target_pairs={{1,8},{8,1},{3,10},{10,3},{5,12},{12,5},{7,14},{14,7},{17,24},{24,... | collective-permute-start | bytes 847880 | tf_op jit(solution)/shard_map/ppermute | solution.py:24
  267.8 18.7 %collective-permute-start.48 = (bf16[160,1024]{1,0:T(8,128)(2,1)S(1)}, bf16[160,1024]{1,0:T(8,128)(2,1)S(1)}, u32[]{:S(2)}, u32[]{:S(2)}) collective-permute-start(bf16[160,1024]{1,0:T(8,128)(2,1)S(1)} %get-tuple-element.127), channel_id=1, source_target_pairs={{0,1},{1,16},{16,17},{17,32},{32,33},{33,48},{48,49},{49,64},{64,6... | collective-permute-start | bytes 983048 | tf_op jit(solution)/shard_map/ppermute | solution.py:30
  306.4 9.0 %collective-permute-start.57 = (bf16[256,512]{1,0:T(8,128)(2,1)S(1)}, bf16[256,512]{1,0:T(8,128)(2,1)S(1)}, u32[]{:S(2)}, u32[]{:S(2)}) collective-permute-start(bf16[256,512]{1,0:T(8,128)(2,1)S(1)} %get-tuple-element.145), channel_id=1, source_target_pairs={{0,4},{2,6},{4,0},{6,2},{1,5},{3,7},{5,1},{7,3},{8,12},{10,14},{12... | collective-permute-start | bytes 786440 | tf_op jit(solution)/shard_map/ppermute | solution.py:20
  306.7 13.8 %collective-permute-start.56 = (bf16[256,512]{1,0:T(8,128)(2,1)S(1)}, bf16[256,512]{1,0:T(8,128)(2,1)S(1)}, u32[]{:S(2)}, u32[]{:S(2)}) collective-permute-start(bf16[256,512]{1,0:T(8,128)(2,1)S(1)} %get-tuple-element.146), channel_id=1, source_target_pairs={{0,6},{2,0},{4,2},{6,4},{1,7},{3,1},{5,3},{7,5},{8,14},{10,8},{12,... | collective-permute-start | bytes 786440 | tf_op jit(solution)/shard_map/ppermute | solution.py:20
  308.6 14.1 %collective-permute-start.55 = (bf16[256,512]{1,0:T(8,128)(2,1)S(1)}, bf16[256,512]{1,0:T(8,128)(2,1)S(1)}, u32[]{:S(2)}, u32[]{:S(2)}) collective-permute-start(bf16[256,512]{1,0:T(8,128)(2,1)S(1)} %get-tuple-element.144), channel_id=1, source_target_pairs={{0,2},{2,4},{4,6},{6,0},{1,3},{3,5},{5,7},{7,1},{8,10},{10,12},{12... | collective-permute-start | bytes 786440 | tf_op jit(solution)/shard_map/ppermute | solution.py:20
  309.3 17.4 %collective-permute-start.52 = (bf16[256,512]{1,0:T(8,128)(2,1)S(1)}, bf16[256,512]{1,0:T(8,128)(2,1)S(1)}, u32[]{:S(2)}, u32[]{:S(2)}) collective-permute-start(bf16[256,512]{1,0:T(8,128)(2,1)S(1)} %get-tuple-element.142), channel_id=1, source_target_pairs={{0,4},{2,6},{4,0},{6,2},{1,5},{3,7},{5,1},{7,3},{8,12},{10,14},{12... | collective-permute-start | bytes 786440 | tf_op jit(solution)/shard_map/ppermute | solution.py:20
  311.4 20.3 %collective-permute-start.51 = (bf16[256,512]{1,0:T(8,128)(2,1)S(1)}, bf16[256,512]{1,0:T(8,128)(2,1)S(1)}, u32[]{:S(2)}, u32[]{:S(2)}) collective-permute-start(bf16[256,512]{1,0:T(8,128)(2,1)S(1)} %get-tuple-element.143), channel_id=1, source_target_pairs={{0,6},{2,0},{4,2},{6,4},{1,7},{3,1},{5,3},{7,5},{8,14},{10,8},{12,... | collective-permute-start | bytes 786440 | tf_op jit(solution)/shard_map/ppermute | solution.py:20
  315.4 17.6 %collective-permute-start.50 = (bf16[256,512]{1,0:T(8,128)(2,1)S(1)}, bf16[256,512]{1,0:T(8,128)(2,1)S(1)}, u32[]{:S(2)}, u32[]{:S(2)}) collective-permute-start(bf16[256,512]{1,0:T(8,128)(2,1)S(1)} %get-tuple-element.141), channel_id=1, source_target_pairs={{0,2},{2,4},{4,6},{6,0},{1,3},{3,5},{5,7},{7,1},{8,10},{10,12},{12... | collective-permute-start | bytes 786440 | tf_op jit(solution)/shard_map/ppermute | solution.py:20
  322.8 14.0 %collective-permute-start.58 = (bf16[256,512]{1,0:T(8,128)(2,1)S(1)}, bf16[256,512]{1,0:T(8,128)(2,1)S(1)}, u32[]{:S(2)}, u32[]{:S(2)}) collective-permute-start(bf16[256,512]{1,0:T(8,128)(2,1)S(1)} %fusion.3), channel_id=1, source_target_pairs={{1,8},{8,1},{3,10},{10,3},{5,12},{12,5},{7,14},{14,7},{17,24},{24,... | collective-permute-start | bytes 786440 | tf_op jit(solution)/shard_map/ppermute | solution.py:24
  333.3 9.2 %collective-permute-start.53 = (bf16[256,512]{1,0:T(8,128)(2,1)S(1)}, bf16[256,512]{1,0:T(8,128)(2,1)S(1)}, u32[]{:S(2)}, u32[]{:S(2)}) collective-permute-start(bf16[256,512]{1,0:T(8,128)(2,1)S(1)} %fusion.7), channel_id=1, source_target_pairs={{1,8},{8,1},{3,10},{10,3},{5,12},{12,5},{7,14},{14,7},{17,24},{24,... | collective-permute-start | bytes 786440 | tf_op jit(solution)/shard_map/ppermute | solution.py:24
  (46 other events, 500.9 us)
Sparse Core Ops, SparseCore 0:
  9.7 88.9 all-gather.6
  118.3 107.5 all-gather.8
  228.0 60.2 all-gather.10
